TPU v7x, 128 devices: a whole 4x4x4 slice. The times are simulated.
128 devices in a mesh: ctx: 4 (over z_hi, core), exp: 32 (over x, y, z_lo).
Axes of the slice: x: 4, y: 4, z: 4 (z_hi: 2, z_lo: 2; z = z_hi * 2 + z_lo), core: 2. Of those that a mesh axis runs over, the one named last changes fastest.
Arguments:
- resid: bfloat16 [2048, 4096], P(('ctx', 'exp')), may hold values from -6 to 6
- query: bfloat16 [2048, 8192], P('ctx', 'exp'), may hold values from -100 to 100
- keys: bfloat16 [2048, 512], P('ctx'), may hold values from -4 to 4
- values: bfloat16 [2048, 512], P('ctx'), may hold values from -8 to 8
- out_weight: bfloat16 [8192, 4096], P('exp'), may hold values from -0.0625 to 0.0625
- post_gain: float32 [4096], replicated, may hold values from 0.5 to 1.5
- route_idx: int32 [2048, 8], replicated, may hold values from 0 to 31, all different within a row; in each aligned block of 16 rows (0 to 15, 16 to 31, ...) at most 8 rows name the same one
- gates: float32 [2048, 8], P(('ctx', 'exp')), may hold values from 0.05 to 0.5
- w_gate: bfloat16 [32, 4096, 1536], P('exp', None, 'ctx'), may hold values from -0.09375 to 0.09375
- w_up: bfloat16 [32, 4096, 1536], P('exp', None, 'ctx'), may hold values from -0.09375 to 0.09375
- w_down: bfloat16 [32, 1536, 4096], P('exp', 'ctx'), may hold values from -0.15625 to 0.15625
Outputs:
- mixed: bfloat16 [2048, 4096], P(('ctx', 'exp'))
- attn_out: float32 [2048, 4096], P(('ctx', 'exp'))
- gram: float32 [32, 1536, 1536], P('exp', 'ctx')
Inputs may be any that keep to these rules, and one draw needn't show every extreme that they name: `route_idx`: in each aligned block of 16 rows (the rows of one device) no expert is named by more than 8 rows, a bound that some block reaches.
All inputs are finite; a program needn't handle non-finite values.
Results may differ from a plain program's by a relative error of at most 0.03.
Values may be sent and summed in bfloat16 or wider, within the bound.
A program may use at most 128 MiB of HBM per device.

v0:
```python
import math

import jax
import jax.numpy as jnp
from jax import lax
from jax.sharding import PartitionSpec as P

QUERY_HEADS = 64
KEY_VALUE_HEADS = 4
HEAD_SIZE = 128


def block_slots(route_idx, block, tok_dev, experts, capacity):
    mine = lax.dynamic_slice_in_dim(route_idx, block * tok_dev, tok_dev, 0)
    top_k = mine.shape[1]
    flat = mine.reshape(-1)
    count_rows = flat.shape[0]
    onehot = (flat[:, None] == jnp.arange(experts, dtype=jnp.int32)[None, :]).astype(jnp.float32)
    lower = (jnp.arange(count_rows)[:, None] > jnp.arange(count_rows)[None, :]).astype(jnp.float32)
    before = jnp.dot(lower, onehot, precision=lax.Precision.HIGHEST)
    ranking = jnp.sum(onehot * before, axis=1).astype(jnp.int32).reshape(tok_dev, top_k)
    slots = mine * capacity + ranking
    places = jnp.arange(experts * capacity, dtype=jnp.int32)
    routing = jnp.any(slots[None, :, :] == places[:, None, None], axis=2).astype(jnp.bfloat16)
    return (slots, routing)


def local(
    resid, query, keys, values, out_weight, post_gain, route_idx, gates, w_gate, w_up, w_down
):
    n_exp = lax.axis_size("exp")
    ctx_pos = lax.axis_index("ctx")
    exp_pos = lax.axis_index("exp")
    span = query.shape[0]
    heads = query.shape[1] // HEAD_SIZE
    head_group = QUERY_HEADS // KEY_VALUE_HEADS
    scale = 1.0 / math.sqrt(HEAD_SIZE)
    kv_head = exp_pos * heads // head_group
    key_part = lax.dynamic_slice_in_dim(keys, kv_head * HEAD_SIZE, HEAD_SIZE, 1)
    value_part = lax.dynamic_slice_in_dim(values, kv_head * HEAD_SIZE, HEAD_SIZE, 1)
    q_heads = query.reshape(span, heads, HEAD_SIZE)
    q_place = ctx_pos * span + jnp.arange(span, dtype=jnp.int32)
    peak = jnp.full((heads, span), -1e30, jnp.float32)
    accum = jnp.zeros((span, heads, HEAD_SIZE), jnp.float32)
    k_piece = lax.all_gather(key_part, "ctx", axis=0, tiled=True)
    v_piece = lax.all_gather(value_part, "ctx", axis=0, tiled=True)
    scores = jnp.einsum("qhd,kd->hqk", q_heads, k_piece, preferred_element_type=jnp.float32) * scale
    k_place = jnp.arange(k_piece.shape[0], dtype=jnp.int32)
    allowed = (q_place[:, None] >= k_place[None, :])[None]
    scores = jnp.where(allowed, scores, -1e30)
    new_peak = jnp.maximum(peak, jnp.max(scores, axis=2))
    weights = jnp.where(allowed, jnp.exp(scores - new_peak[:, :, None]), 0.0).astype(jnp.bfloat16)
    fade = jnp.exp(peak - new_peak)
    total = jnp.sum(weights.astype(jnp.float32), axis=2)
    update = jnp.einsum("hqk,kd->qhd", weights, v_piece, preferred_element_type=jnp.float32)
    accum = accum * fade.T[:, :, None] + update
    peak, total, accum = (new_peak, total, accum)
    head_rows = (accum / total.T[:, :, None]).astype(jnp.bfloat16).reshape(span, heads * HEAD_SIZE)
    tok_dev = resid.shape[0]
    rows = head_rows
    attn_out = lax.psum_scatter(
        jnp.dot(rows, out_weight, preferred_element_type=jnp.float32).astype(jnp.bfloat16),
        "exp",
        scatter_dimension=0,
        tiled=True,
    ).astype(jnp.float32)
    stream = (resid.astype(jnp.float32) + attn_out).astype(jnp.bfloat16)
    stream_f = stream.astype(jnp.float32)
    normed = (
        stream_f
        * lax.rsqrt(jnp.mean(stream_f * stream_f, axis=1, keepdims=True) + 1e-06)
        * post_gain
    ).astype(jnp.bfloat16)
    top_k = route_idx.shape[1]
    capacity = max(2, 2 * tok_dev * top_k // n_exp)
    width = normed.shape[1]
    ff_part = w_gate.shape[2]
    block = ctx_pos * n_exp + exp_pos
    slots, routing = block_slots(route_idx, block, tok_dev, n_exp, capacity)
    send = (
        jnp.dot(routing, normed, preferred_element_type=jnp.float32)
        .astype(jnp.bfloat16)
        .reshape(n_exp, capacity, width)
    )
    received = lax.all_to_all(send, "exp", split_axis=0, concat_axis=0, tiled=True)
    rows = lax.all_gather(received, "ctx", axis=0, tiled=True)
    flat = rows.reshape(-1, rows.shape[-1])
    gate = jnp.dot(flat, w_gate[0], preferred_element_type=jnp.float32)
    upper = jnp.dot(flat, w_up[0], preferred_element_type=jnp.float32)
    hidden = (jax.nn.silu(gate) * upper).astype(jnp.bfloat16).reshape(rows.shape[:-1] + (ff_part,))
    hidden_rows = hidden.reshape(-1, ff_part)
    hidden_full = lax.all_gather(hidden_rows, "ctx", axis=1, tiled=True)
    count = jnp.sum(jnp.any(route_idx == exp_pos, axis=1).astype(jnp.float32))
    gram = (
        lax.dot_general(
            hidden_rows, hidden_full, (((0,), (0,)), ((), ())), preferred_element_type=jnp.float32
        )
        / count
    )
    rows = hidden_rows
    expert_out = lax.psum_scatter(
        jnp.dot(rows, w_down[0], preferred_element_type=jnp.float32).astype(jnp.bfloat16),
        "ctx",
        scatter_dimension=0,
        tiled=True,
    )
    outgoing = expert_out.reshape(n_exp, capacity, width)
    returned = lax.all_to_all(outgoing, "exp", split_axis=0, concat_axis=0, tiled=True).reshape(
        n_exp * capacity, width
    )
    selected_experts = returned[slots]
    routed = jnp.sum(gates[:, :, None] * selected_experts.astype(jnp.float32), axis=1)
    mixed = (stream_f + routed).astype(jnp.bfloat16)
    return (mixed, attn_out, gram[None])


def solution(mesh):
    placed = (
        P(("ctx", "exp"), None),
        P("ctx", "exp"),
        P("ctx", None),
        P("ctx", None),
        P("exp", None),
        P(),
        P(),
        P(("ctx", "exp"), None),
        P("exp", None, "ctx"),
        P("exp", None, "ctx"),
        P("exp", "ctx", None),
    )
    return jax.shard_map(
        local,
        mesh=mesh,
        in_specs=placed,
        out_specs=(P(("ctx", "exp"), None), P(("ctx", "exp"), None), P("exp", "ctx", None)),
        check_vma=False,
    )
```

profile of v0, /device:TPU:1, one launch (start us, length us, event | category | flops | bytes accessed | tf_op | source)
XLA Modules:
  0.0 474.7 jit_solution(9691980715218068902)
XLA Ops:
  7.2 0.0 copy-start
  7.2 0.0 reduce-scatter.3.cloned.1.call-start
  7.2 1.1 constant_dynamic-slice_fusion.1
  8.3 0.1 copy.35
  8.4 11.4 %all_gather.13 = bf16[2048,128]{0,1:T(8,128)(2,1)} all-gather(bf16[512,128]{0,1:T(8,128)(2,1)S(1)} %copy.35), channel_id=1, replica_groups=mesh['ctx'=4,'exp'=32] {'ctx'}, dimensions={0}, use_global_device_ids=true | all-gather | bytes 655360 | tf_op jit(solution)/shard_map/all_gather | solution.py:46
  19.8 0.8 iota_compare_fusion
  20.6 0.9 constant_dynamic-slice_fusion.2
  21.6 8.8 %all_gather.12 = bf16[2048,128]{1,0:T(8,128)(2,1)S(1)} all-gather(bf16[512,128]{1,0:T(8,128)(2,1)S(1)} %constant_dynamic-slice_fusion.2), channel_id=1, replica_groups=mesh['ctx'=4,'exp'=32] {'ctx'}, dimensions={0}, use_global_device_ids=true | all-gather | bytes 655360 | tf_op jit(solution)/shard_map/all_gather | solution.py:45
  30.4 2.8 fusion.4
  33.2 2.3 convert_reduce_fusion
  35.4 0.0 copy-start.1
  35.4 2.3 fusion.17
  37.8 0.0 copy-start.4
  37.8 0.0 copy-start.3
  37.8 0.0 copy-start.5
  37.8 3.2 convolution_convert_fusion.1
  41.0 0.0 reduce-scatter.3.cloned.1.call-update
  41.0 0.0 all-gather.3.cloned.1.call-start
  41.1 0.1 constant_dynamic-slice_fusion
  41.2 0.1 copy.36
  41.2 0.1 eq.34
  41.3 0.2 fusion.18
  41.5 0.1 convert_element_type.64
  41.6 0.1 fusion.31
  41.7 145.7 %reduce-scatter.3.cloned.1.call-done = bf16[16,4096]{1,0:T(8,128)(2,1)} async-done(((bf16[512,4096]{1,0:T(8,128)(2,1)}), bf16[16,4096]{1,0:T(8,128)(2,1)}) %reduce-scatter.3.cloned.1.call-update) | async-done | bytes 131088 | tf_op jit(solution)/shard_map/reduce_scatter | solution.py:61
  187.5 1.8 fusion.22
  189.2 0.8 fusion.5
  190.0 22.2 %all_to_all.10 = bf16[32,8,4096]{2,1,0:T(8,128)(2,1)} all-to-all(bf16[32,8,4096]{2,1,0:T(8,128)(2,1)S(1)} %fusion.5), channel_id=1, replica_groups=mesh['ctx'=4,'exp'=32] {'exp'}, dimensions={0} | all-to-all | bytes 4194304 | tf_op jit(solution)/shard_map/all_to_all | solution.py:85
  212.2 0.0 all-gather.3.cloned.1.call-update
  212.2 0.2 reduce-scatter.5.cloned.1.call-start
  212.5 91.2 %all-gather.3.cloned.1.call-done = bf16[128,8,4096]{2,1,0:T(8,128)(2,1)} async-done(((bf16[32,8,4096]{2,1,0:T(8,128)(2,1)}), bf16[128,8,4096]{2,1,0:T(8,128)(2,1)}) %all-gather.3.cloned.1.call-update) | async-done | bytes 8388624 | tf_op jit(solution)/shard_map/all_gather | solution.py:86
  303.7 8.0 %fusion.2 = f32[1024,384]{1,0:T(8,128)S(1)} fusion(bf16[128,8,4096]{2,1,0:T(8,128)(2,1)} %all-gather.3.cloned.1.call-done, bf16[1,4096,384]{2,1,0:T(8,128)(2,1)} %param.19), kind=kOutput, calls=%fused_computation.3 | convolution fusion | flops 3221225472 | bytes 13107200 | tf_op jit(solution)/shard_map/dot_general | solution.py:88
  311.7 5.5 %multiply_convert_fusion = bf16[1024,384]{1,0:T(8,128)(2,1)} fusion(f32[1024,384]{1,0:T(8,128)S(1)} %fusion.2, bf16[1,4096,384]{2,1,0:T(8,128)(2,1)S(1)} %copy-done.8, bf16[128,8,4096]{2,1,0:T(8,128)(2,1)S(1)} %copy-done.7), kind=kOutput, calls=%fused_computation.21 | convolution fusion | flops 3223584768 | bytes 13893632 | tf_op jit(solution)/shard_map/dot_general | solution.py:89
  317.1 7.8 %convolution_convert_fusion = bf16[1024,4096]{1,0:T(8,128)(2,1)} fusion(bf16[1024,384]{1,0:T(8,128)(2,1)} %multiply_convert_fusion, bf16[1,384,4096]{2,1,0:T(8,128)(2,1)S(1)} %copy-done), kind=kOutput, calls=%fused_computation.8 | convolution fusion | flops 3225419776 | bytes 12320768 | tf_op jit(solution)/shard_map/dot_general | solution.py:102
  324.9 0.0 reduce-scatter.5.cloned.1.call-update
  324.9 0.0 copy-start.6
  325.0 0.0 all-gather.5.cloned.1.call-start
  325.0 0.5 all-gather.5.cloned.1.call-update
  325.5 77.1 %reduce-scatter.5.cloned.1.call-done = bf16[256,4096]{1,0:T(8,128)(2,1)} async-done(((bf16[1024,4096]{1,0:T(8,128)(2,1)}), bf16[256,4096]{1,0:T(8,128)(2,1)}) %reduce-scatter.5.cloned.1.call-update) | async-done | bytes 2097168 | tf_op jit(solution)/shard_map/reduce_scatter | solution.py:101
  402.6 7.0 %all-to-all-start.1 = ((bf16[32,8,4096]{2,1,0:T(8,128)(2,1)}), bf16[32,8,4096]{2,1,0:T(8,128)(2,1)}, u32[]{:S(2)}, u32[]{:S(2)}) async-start(bf16[32,8,4096]{2,1,0:T(8,128)(2,1)} %bitcast.71), calls=%async_computation.3 | async-start | bytes 4194304 | tf_op jit(solution)/shard_map/all_to_all | solution.py:108
  409.7 0.1 reshape.75
  409.8 0.1 copy.32
  409.9 0.6 convert_reduce_fusion.1
  410.5 44.3 %all-gather.5.cloned.1.call-done = bf16[1024,1536]{1,0:T(8,128)(2,1)} async-done(((bf16[1024,384]{1,0:T(8,128)(2,1)}), bf16[1024,1536]{1,0:T(8,128)(2,1)}) %all-gather.5.cloned.1.call-update) | async-done | bytes 3145744 | tf_op jit(solution)/shard_map/all_gather | solution.py:92
  454.8 5.6 %fusion.9 = f32[1,384,1536]{2,1,0:T(8,128)} fusion(bf16[1024,384]{1,0:T(8,128)(2,1)} %multiply_convert_fusion, bf16[1024,1536]{1,0:T(8,128)(2,1)} %all-gather.5.cloned.1.call-done, f32[]{:T(128)} %convert_reduce_fusion.1), kind=kOutput, calls=%fused_computation.18 | convolution fusion | flops 1208549376 | bytes 6291460 | tf_op jit(solution)/shard_map/dot_general | solution.py:95
  460.4 5.0 %gather_fusion = bf16[128,4096]{1,0:T(8,128)(2,1)} fusion(bf16[256,4096]{1,0:T(8,128)(2,1)} %bitcast.13, s32[1024]{0:T(1024)S(1)} %pad_clamp_fusion), kind=kCustom, calls=%fused_computation | custom fusion | bytes 2097664 | tf_op jit(solution)/shard_map/gather | solution.py:111
  465.4 2.0 fusion.10
  467.5 0.7 fusion.25
  (20 shorter events, 0.1 us)
Async XLA Ops:
  7.2 310.0 %copy-start = (bf16[1,384,4096]{2,1,0:T(8,128)(2,1)S(1)}, bf16[1,384,4096]{2,1,0:T(8,128)(2,1)}, u32[]{:S(2)}) copy-start(bf16[1,384,4096]{2,1,0:T(8,128)(2,1)} %param.21) | copy-start | bytes 9437188
  7.2 180.3 %reduce-scatter.3.cloned.1.call-start = ((), (), s32[]{:S(2)}) async-start(), calls=%async_computation.4 | async-start | bytes 4325376 | tf_op jit(solution)/shard_map/reduce_scatter | solution.py:61
  33.1 2.3 copy-start.2
  35.4 2.3 copy-start.1
  37.8 3.3 copy-start.4
  37.8 149.7 %copy-start.3 = (bf16[16,4096]{1,0:T(8,128)(2,1)S(1)}, bf16[16,4096]{1,0:T(8,128)(2,1)}, u32[]{:S(2)}) copy-start(bf16[16,4096]{1,0:T(8,128)(2,1)} %param.11) | copy-start | bytes 393220
  37.8 151.4 %copy-start.5 = (f32[4096]{0:T(1024)S(1)}, f32[4096]{0:T(1024)}, u32[]{:S(2)}) copy-start(f32[4096]{0:T(1024)} %param.16) | copy-start | bytes 49156
  41.0 262.7 %all-gather.3.cloned.1.call-start = ((), (), s32[]{:S(2)}) async-start(), calls=%async_computation.5 | async-start | bytes 10485760 | tf_op jit(solution)/shard_map/all_gather | solution.py:86
  212.2 190.4 %reduce-scatter.5.cloned.1.call-start = ((), (), s32[]{:S(2)}) async-start(), calls=%async_computation.6 | async-start | bytes 10485760 | tf_op jit(solution)/shard_map/reduce_scatter | solution.py:101
  303.7 8.0 %copy-start.7 = (bf16[128,8,4096]{2,1,0:T(8,128)(2,1)S(1)}, bf16[128,8,4096]{2,1,0:T(8,128)(2,1)}, u32[]{:S(2)}) copy-start(bf16[128,8,4096]{2,1,0:T(8,128)(2,1)} %all-gather.3.cloned.1.call-done) | copy-start | bytes 25165828
  303.7 8.0 %copy-start.8 = (bf16[1,4096,384]{2,1,0:T(8,128)(2,1)S(1)}, bf16[1,4096,384]{2,1,0:T(8,128)(2,1)}, u32[]{:S(2)}) copy-start(bf16[1,4096,384]{2,1,0:T(8,128)(2,1)} %param.20) | copy-start | bytes 9437188
  324.9 84.8 %copy-start.6 = (f32[16,8]{0,1:T(8,128)S(1)}, f32[16,8]{0,1:T(8,128)}, u32[]{:S(2)}) copy-start(f32[16,8]{0,1:T(8,128)} %param.18) | copy-start | bytes 1540
  325.0 129.8 %all-gather.5.cloned.1.call-start = ((), (), s32[]{:S(2)}) async-start(), calls=%async_computation.7 | async-start | bytes 3932160 | tf_op jit(solution)/shard_map/all_gather | solution.py:92
  402.6 57.7 %all-to-all-start.1 = ((bf16[32,8,4096]{2,1,0:T(8,128)(2,1)}), bf16[32,8,4096]{2,1,0:T(8,128)(2,1)}, u32[]{:S(2)}, u32[]{:S(2)}) async-start(bf16[32,8,4096]{2,1,0:T(8,128)(2,1)} %bitcast.71), calls=%async_computation.3 | async-start | bytes 4194304 | tf_op jit(solution)/shard_map/all_to_all | solution.py:108
Sparse Core Ops, SparseCore 0:
  41.1 146.2 reduce-scatter.2
  212.4 91.2 all-gather.2
  325.1 77.5 reduce-scatter.4
  404.3 50.4 all-gather.4
where the time goes:
time: 475 us
  waiting for transfers between devices  359 us (76%)
  blocking collectives  42.4 us (9%)
  matrix products  36 us (8%)
  between operations  14 us (3%)
  other arithmetic  8.37 us (2%)
  local copies, waits for them, and re-layouts  7.68 us (2%)
  starting transfers between devices  7.38 us (2%)
    reduce_scatter x1, waiting for transfers between devices, local(): lax.psum_scatter(jnp.dot(rows, out_weight, preferred_element_type=jnp.flo...  146 us
    all_gather x1, waiting for transfers between devices, local(): rows = lax.all_gather(received, 'ctx', axis=0, tiled=True)  91.2 us
    reduce_scatter x1, waiting for transfers between devices, local(): lax.psum_scatter(jnp.dot(rows, w_down[0], preferred_element_type=jnp.floa...  77.1 us
    all_gather x1, waiting for transfers between devices, local(): hidden_full = lax.all_gather(hidden_rows, 'ctx', axis=1, tiled=True)  44.3 us
    all_to_all x1, blocking collectives, local(): lax.all_to_all(send, 'exp', split_axis=0, concat_axis=0, tiled=True)  22.2 us
    all_gather x1, blocking collectives, local(): v_piece = lax.all_gather(value_part, 'ctx', axis=0, tiled=True)  11.4 us
  transfers between devices with their start and end apart: 5, of which 4 were waited for; matrix products, arithmetic and copies ran while one was open for 1% of the time, Pallas kernels for 0%

commit v1 on v0

v1 whole, which is shorter than its diff:
```python
import functools
import math

import jax
import jax.numpy as jnp
from jax import lax
from jax.experimental import pallas as pl
from jax.experimental.pallas import tpu as pltpu
from jax.sharding import PartitionSpec as P

QUERY_HEADS = 64
EXPERTS = 32
KEY_VALUE_HEADS = 4
HEAD_SIZE = 128
D = 4096
FF = 1536
FFS = 384
HALF = D // 2
QUART = D // 4
MESH = pl.DeviceIdType.MESH
BF = jnp.bfloat16
F32 = jnp.float32

RS_ORDER = ((0, 2, 1, 3, 4), (2, 1, 3, 0, 4), (1, 3, 0, 2, 4), (3, 0, 2, 1, 4))
CYCLE = (0, 2, 4, 1, 3, 5)
WIDTHS = (384, 384, 384, 384, 384, 256)
USED = (384, 384, 384, 384, 256, 256)
OFFS = (0, 384, 768, 1152, 1536, 1792)
WIDE = HALF + 128
GRAY = (0, 1, 3, 2)
ZMAP = ((0, 0), (1, 0), (1, 1), (0, 1))
FULL = slice(None)


def block_bits(i, n):
    return [(i // (2 ** (n - 1 - j))) % 2 for j in range(n)]


def kernel(
    h_ref, ow_ref, resid_ref, gain_ref, gate_ref, sel_ref, exp_ref, wg_ref, wu_ref, wd_ref,
    mixed_ref, attn_ref, gram_ref,
    p1, r10, r11, r12, r13, r14, norm, stream, csh, x0, x1, x2, x3, x4, x5,
    wgk, wuk, wgs, wus, wdq, xs, psend, precv, hall, p2, r20, r21, r22, r23, r24, fsend, frecv,
    s1s, s1r, wss, wsr, lsem, ccs, ccr, ags, agr, pss, psr, hss, hsr, s2s, s2r, fss, fsr,
):
    c = lax.axis_index("ctx")
    e = lax.axis_index("exp")
    x, y, zl, zh, k = e // 8, (e // 2) % 4, e % 2, c // 2, c % 2

    def dev(x_, y_, zl_, zh_, k_):
        return (zh_ * 2 + k_, x_ * 8 + y_ * 2 + zl_)

    def flip1(v):
        return v + 1 - 2 * (v % 2)

    peer_x = (dev(3 - x, y, zl, zh, k), dev(flip1(x), y, zl, zh, k))
    peer_y = (dev(x, 3 - y, zl, zh, k), dev(x, flip1(y), zl, zh, k))
    peer_z1 = dev(x, y, 1 - zl, zh, k)
    peer_z3 = dev(x, y, 1 - zl, 1 - zh, k)
    sib = dev(x, y, zl, zh, 1 - k)
    far = dev(x, y, zl, 1 - zh, k)
    farsib = dev(x, y, zl, 1 - zh, 1 - k)
    rs_peer = (peer_x[0], peer_x[1], peer_y[0], peer_y[1], peer_z1)
    ag_peer = (peer_x[0], peer_x[1], peer_y[0], peer_y[1], peer_z3, peer_z1)
    xb1, yb1 = x // 2, y // 2
    own5 = (xb1, (xb1 + x % 2) % 2, yb1, (yb1 + y % 2) % 2, zl)
    own6 = own5[:4] + (zh, (zh + zl) % 2)

    barrier = pltpu.get_barrier_semaphore()
    partners = list(ag_peer) + [sib, far, farsib]
    for p in partners:
        pl.semaphore_signal(barrier, inc=1, device_id=p, device_id_type=MESH)
    pl.semaphore_wait(barrier, len(partners))

    def remote(src, dst, ss, rs, to):
        return pltpu.make_async_remote_copy(
            src_ref=src, dst_ref=dst, send_sem=ss, recv_sem=rs, device_id=to, device_id_type=MESH
        )

    def rs_index(f, s, bit):
        order = RS_ORDER[f]
        idx = [FULL] * 5
        for d in order[:s]:
            idx[d] = own5[d]
        idx[order[s]] = bit
        return tuple(idx)

    def rs_copy(buf, recv, ss, rs, f, s):
        d = RS_ORDER[f][s]
        return remote(
            buf.at[(f,) + rs_index(f, s, 1 - own5[d])], recv[s].at[f], ss.at[f, s], rs.at[f, s], rs_peer[d]
        )

    def rs_add(buf, recv, f, s):
        order = RS_ORDER[f]
        left = sorted(order[s + 1 :])
        n = len(left)

        def one(i):
            bits = block_bits(i, n)
            idx = list(own5)
            for d, b in zip(left, bits):
                idx[d] = b
            idx = (f,) + tuple(idx)
            got = recv[s][(f,) + tuple(bits)]
            buf[idx] = (buf[idx].astype(F32) + got.astype(F32)).astype(BF)

        pl.loop(0, 2**n)(one)

    recv1 = (r10, r11, r12, r13, r14)
    recv2 = (r20, r21, r22, r23, r24)

    def project(f, bit):
        idx = rs_index(f, 0, bit)
        rows = h_ref[idx].reshape(256, 256)
        for t in range(2):
            cols = f * 1024 + t * 512
            out = jnp.dot(rows, ow_ref[:, cols : cols + 512], preferred_element_type=F32)
            p1[(f,) + idx + (FULL, slice(t * 512, t * 512 + 512))] = out.astype(BF).reshape(2, 2, 2, 2, 16, 512)

    first = []
    for f in range(4):
        project(f, 1 - own5[RS_ORDER[f][0]])
        cp = rs_copy(p1, recv1, s1s, s1r, f, 0)
        cp.start()
        first.append(cp)

    other = pl.ds(pl.multiple_of((1 - k) * HALF, HALF), HALF)
    mine = pl.ds(pl.multiple_of(k * HALF, HALF), HALF)
    own_rows = pl.ds(pl.multiple_of(c * FFS, FFS), FFS)

    def quarter(cc):
        return pl.ds(pl.multiple_of(cc * QUART, QUART), QUART)

    weight_copies = [
        remote(wg_ref.at[other], wgs, wss.at[0], wsr.at[0], sib),
        remote(wu_ref.at[other], wus, wss.at[1], wsr.at[1], sib),
        remote(wd_ref.at[:, quarter(zh * 2 + 1 - k)], wdq.at[own_rows], wss.at[2], wsr.at[2], sib),
        remote(wd_ref.at[:, quarter((1 - zh) * 2 + k)], wdq.at[own_rows], wss.at[3], wsr.at[3], far),
        remote(wd_ref.at[:, quarter((1 - zh) * 2 + 1 - k)], wdq.at[own_rows], wss.at[4], wsr.at[4], farsib),
    ]
    local_copies = [
        pltpu.make_async_copy(wg_ref.at[mine], wgk, lsem.at[0]),
        pltpu.make_async_copy(wu_ref.at[mine], wuk, lsem.at[1]),
        pltpu.make_async_copy(wd_ref.at[:, quarter(c)], wdq.at[own_rows], lsem.at[2]),
    ]
    for cp in weight_copies + local_copies:
        cp.start()

    for f in range(4):
        project(f, own5[RS_ORDER[f][0]])

    def finish_rs(buf, recv, ss, rs, first):
        last = list(first)
        for s in range(4):
            for f in range(4):
                last[f].wait()
                rs_add(buf, recv, f, s)
                last[f] = rs_copy(buf, recv, ss, rs, f, s + 1)
                last[f].start()
        out = []
        for f in range(4):
            last[f].wait()
            out.append(buf[(f,) + own5].astype(F32) + recv[4][f].astype(F32))
        return out

    parts = finish_rs(p1, recv1, s1s, s1r, first)

    squares = jnp.zeros((16, 1), F32)
    for f in range(4):
        cols = slice(f * 1024, f * 1024 + 1024)
        attn_ref[:, cols] = parts[f]
        st = (resid_ref[:, cols].astype(F32) + parts[f]).astype(BF)
        stream[:, cols] = st
        sf = st.astype(F32)
        squares = squares + jnp.sum(sf * sf, axis=1, keepdims=True)
    inv = lax.rsqrt(squares / D + 1e-06)
    for f in range(4):
        cols = slice(f * 1024, f * 1024 + 1024)
        out = (stream[:, cols].astype(F32) * inv * gain_ref[:, cols]).astype(BF)
        norm[f // 2, :, (f % 2) * 1024 : (f % 2) * 1024 + 1024] = out
    gates = gate_ref[...]
    top = gates.astype(BF)
    rest = gates - top.astype(F32)
    middle = rest.astype(BF)
    low = (rest - middle.astype(F32)).astype(BF)
    lane = lax.broadcasted_iota(jnp.int32, (16, 128), 1)
    gates = jnp.where(lane < EXPERTS, top.astype(F32), jnp.where(lane < 2 * EXPERTS, middle.astype(F32), low.astype(F32)))
    for i in range(2):
        norm[i, :, HALF:] = gates.astype(BF)

    xf = (x0, x1, x2, x3, x4, x5)
    swap = remote(norm.at[1 - k], csh, ccs.at[0], ccr.at[0], sib)
    swap.start()
    own_tok = pl.ds(pl.multiple_of(k * 16, 16), 16)
    sib_tok = pl.ds(pl.multiple_of((1 - k) * 16, 16), 16)
    for f in range(6):
        xf[f][own6 + (own_tok, slice(0, USED[f]))] = norm[k, :, OFFS[f] : OFFS[f] + USED[f]]
    x4[own6 + (own_tok, slice(256, 384))] = norm[k, :, HALF:]
    swap.wait()
    for f in range(6):
        xf[f][own6 + (sib_tok, slice(0, USED[f]))] = csh[:, OFFS[f] : OFFS[f] + USED[f]]
    x4[own6 + (sib_tok, slice(256, 384))] = csh[:, HALF:]

    def ag_copy(f, s):
        done = [CYCLE[(f + t) % 6] for t in range(s)]
        d = CYCLE[(f + s) % 6]
        idx = tuple(FULL if j in done else own6[j] for j in range(6))
        return remote(xf[f].at[idx], xf[f].at[idx], ags.at[f, s], agr.at[f, s], ag_peer[d])

    last = []
    for f in range(6):
        cp = ag_copy(f, 0)
        cp.start()
        last.append(cp)
    for s in range(1, 6):
        for f in range(6):
            last[f].wait()
            last[f] = ag_copy(f, s)
            last[f].start()
    for f in range(6):
        last[f].wait()

    def select(g):
        b = block_bits(g, 3)
        pick = sel_ref[g]
        rows = pl.ds(pl.multiple_of(g * 128, 128), 128)
        for f in range(6):
            block = xf[f][tuple(b)].reshape(256, WIDTHS[f])[:, : USED[f]]
            xs[rows, OFFS[f] : OFFS[f] + USED[f]] = jnp.dot(pick, block, preferred_element_type=F32).astype(BF)

    pl.loop(0, 8)(select)
    for cp in weight_copies + local_copies:
        cp.wait()

    def partial_copy(m):
        return remote(psend.at[m], precv.at[m], pss.at[m], psr.at[m], sib)

    def other_units(m):
        a = xs[pl.ds(pl.multiple_of(m * 256, 256), 256), :]
        psend[m, :, :FFS] = jnp.dot(a, wgs[...], preferred_element_type=F32).astype(BF)
        psend[m, :, FFS:] = jnp.dot(a, wus[...], preferred_element_type=F32).astype(BF)
        partial_copy(m).start()

    pl.loop(0, 4)(other_units)

    def hidden_cols(cc):
        return pl.ds(pl.multiple_of(cc * FFS, 128), FFS)

    def hidden_copy(m, cc, kind, to):
        part = hall.at[pl.ds(pl.multiple_of(m * 256, 256), 256), hidden_cols(cc)]
        return remote(part, part, hss.at[kind, m], hsr.at[kind, m], to)

    def own_units(m):
        rows = pl.ds(pl.multiple_of(m * 256, 256), 256)
        a = xs[rows, :]
        gate = jnp.dot(a, wgk[...], preferred_element_type=F32)
        upper = jnp.dot(a, wuk[...], preferred_element_type=F32)
        partial_copy(m).wait()
        gate = gate + precv[m, :, :FFS].astype(F32)
        upper = upper + precv[m, :, FFS:].astype(F32)
        hall[rows, hidden_cols(c)] = (gate / (1.0 + jnp.exp(-gate)) * upper).astype(BF)
        hidden_copy(m, c, 0, far).start()
        hidden_copy(m, c, 1, sib).start()

    pl.loop(0, 4)(own_units)
    far_c = (1 - zh) * 2 + k

    def forward(m):
        hidden_copy(m, c, 0, far).wait()
        hidden_copy(m, far_c, 2, sib).start()

    pl.loop(0, 4)(forward)

    def down(m):
        hidden_copy(m, c, 1, sib).wait()
        hidden_copy(m, far_c, 2, sib).wait()
        rows = pl.ds(pl.multiple_of(m * 256, 256), 256)
        a = hall[rows, :]
        b1, b0 = m // 2, m % 2
        lane = lax.broadcasted_iota(jnp.int32, (256, 128), 1)
        mine = jnp.logical_or(lane == e, jnp.logical_or(lane == e + EXPERTS, lane == e + 2 * EXPERTS))
        weights = []
        for g in range(2):
            block = x4[b1, b0, g].reshape(256, 384)[:, 256:].astype(F32)
            weights.append(jnp.sum(jnp.where(mine, block, 0.0), axis=1, keepdims=True))
        for f in range(4):
            cols = slice(f * 256, f * 256 + 256)
            out = jnp.dot(a, wdq[:, cols], preferred_element_type=F32).astype(BF)
            for g in range(2):
                tok = jnp.dot(exp_ref[m * 2 + g], out[g * 128 : g * 128 + 128], preferred_element_type=F32)
                tok = (tok * weights[g]).astype(BF)
                for yb in range(2):
                    for j in range(4):
                        zlo, zhi = ZMAP[j]
                        at = (yb * 4 + j) * 32
                        p2[f, b1, b0, g, yb, zlo, zhi * 32 : zhi * 32 + 32, :] = tok[at : at + 32]

    pl.loop(0, 4)(down)

    first = []
    for f in range(4):
        cp = rs_copy(p2, recv2, s2s, s2r, f, 0)
        cp.start()
        first.append(cp)

    def gram(j):
        cols = pl.ds(pl.multiple_of(j * 256, 256), 256)
        gram_ref[:, cols] = lax.dot_general(
            hall[:, hidden_cols(c)], hall[:, cols], (((0,), (0,)), ((), ())), preferred_element_type=F32
        )

    pl.loop(0, 6)(gram)

    parts = finish_rs(p2, recv2, s2s, s2r, first)
    for f in range(4):
        cols = slice(f * 256, f * 256 + 256)
        fsend[:, :, cols] = parts[f].astype(BF).reshape(4, 16, 256)
    final = []
    for i, (cc, to) in enumerate(
        ((zh * 2 + 1 - k, sib), ((1 - zh) * 2 + k, far), ((1 - zh) * 2 + 1 - k, farsib))
    ):
        cp = remote(fsend.at[cc], frecv.at[c], fss.at[i], fsr.at[i], to)
        cp.start()
        final.append(cp)
    frecv[c] = fsend[c]
    for cp in final:
        cp.wait()
    for cc in range(4):
        cols = slice(cc * QUART, cc * QUART + QUART)
        mixed_ref[:, cols] = (stream[:, cols].astype(F32) + frecv[cc].astype(F32)).astype(BF)


def fused(h, ow, resid, gain, gate, sel, exp, wg, wu, wd):
    dma = pltpu.SemaphoreType.DMA
    vm = pl.BlockSpec(memory_space=pltpu.VMEM)
    hbm = pl.BlockSpec(memory_space=pl.ANY)
    two = (2,) * 6

    def rs_scratch(rows, cols):
        out = [pltpu.VMEM((4,) + (2,) * 5 + (rows, cols), BF)]
        for s in range(5):
            out.append(pltpu.VMEM((4,) + (2,) * (4 - s) + (rows, cols), BF))
        return out

    scratch = (
        rs_scratch(16, 1024)
        + [pltpu.VMEM((2, 16, WIDE), BF), pltpu.VMEM((16, D), BF), pltpu.VMEM((16, WIDE), BF)]
        + [pltpu.VMEM(two + (32, w), BF) for w in WIDTHS]
        + [pltpu.VMEM((HALF, FFS), BF)] * 4
        + [pltpu.VMEM((FF, QUART), BF), pltpu.VMEM((1024, HALF), BF)]
        + [pltpu.VMEM((4, 256, 2 * FFS), BF)] * 2
        + [pltpu.VMEM((1024, FF), BF)]
        + rs_scratch(64, 256)
        + [pltpu.VMEM((4, 16, QUART), BF)] * 2
        + [dma((4, 5)), dma((4, 5)), dma((5,)), dma((5,)), dma((3,)), dma((1,)), dma((1,))]
        + [dma((6, 6)), dma((6, 6)), dma((4,)), dma((4,)), dma((3, 4)), dma((3, 4))]
        + [dma((4, 5)), dma((4, 5)), dma((3,)), dma((3,))]
    )
    return pl.pallas_call(
        kernel,
        out_shape=(
            jax.ShapeDtypeStruct((16, D), BF),
            jax.ShapeDtypeStruct((16, D), F32),
            jax.ShapeDtypeStruct((FFS, FF), F32),
        ),
        in_specs=[vm] * 7 + [hbm] * 3,
        out_specs=(vm, vm, vm),
        scratch_shapes=scratch,
        compiler_params=pltpu.CompilerParams(
            collective_id=0, has_side_effects=True, vmem_limit_bytes=62 * 2**20
        ),
        name="layer",
    )(h, ow, resid, gain, gate, sel, exp, wg, wu, wd)


def gray(a, axis):
    parts = [lax.slice_in_dim(a, i, i + 1, axis=axis) for i in GRAY]
    return jnp.concatenate(parts, axis=axis)


def gathered_order(a):
    rest = a.shape[1:]
    n = len(rest)
    a = a.reshape((2, 2, 4, 4, 2, 16) + rest)
    a = jnp.transpose(a, (2, 3, 0, 4, 1, 5) + tuple(range(6, 6 + n)))
    a = a.reshape((4, 4, 4, 32) + rest)
    for axis in range(3):
        a = gray(a, axis)
    return a.reshape((2048,) + rest)


def attention(query, keys, values):
    ctx_pos = lax.axis_index("ctx")
    exp_pos = lax.axis_index("exp")
    span = query.shape[0]
    heads = query.shape[1] // HEAD_SIZE
    head_group = QUERY_HEADS // KEY_VALUE_HEADS
    scale = 1.0 / math.sqrt(HEAD_SIZE)
    kv_head = exp_pos * heads // head_group
    key_part = lax.dynamic_slice_in_dim(keys, kv_head * HEAD_SIZE, HEAD_SIZE, 1)
    value_part = lax.dynamic_slice_in_dim(values, kv_head * HEAD_SIZE, HEAD_SIZE, 1)
    both = jnp.concatenate([key_part, value_part], axis=1)
    both = lax.all_gather(both, "ctx", axis=0, tiled=True)
    k_piece, v_piece = both[:, :HEAD_SIZE], both[:, HEAD_SIZE:]
    q_heads = query.reshape(span, heads, HEAD_SIZE)
    q_place = ctx_pos * span + jnp.arange(span, dtype=jnp.int32)
    scores = jnp.einsum("qhd,kd->hqk", q_heads, k_piece, preferred_element_type=F32) * scale
    k_place = jnp.arange(k_piece.shape[0], dtype=jnp.int32)
    allowed = (q_place[:, None] >= k_place[None, :])[None]
    scores = jnp.where(allowed, scores, -1e30)
    peak = jnp.max(scores, axis=2)
    weights = jnp.where(allowed, jnp.exp(scores - peak[:, :, None]), 0.0).astype(BF)
    total = jnp.sum(weights.astype(F32), axis=2)
    accum = jnp.einsum("hqk,kd->qhd", weights, v_piece, preferred_element_type=F32)
    return (accum / total.T[:, :, None]).astype(BF).reshape(span, heads * HEAD_SIZE)


def local(
    resid, query, keys, values, out_weight, post_gain, route_idx, gates, w_gate, w_up, w_down
):
    exp_pos = lax.axis_index("exp")
    block = lax.axis_index("ctx") * EXPERTS + exp_pos
    own_idx = lax.dynamic_slice_in_dim(route_idx, block * 16, 16, 0)
    expert = jnp.arange(128, dtype=jnp.int32)
    expert = jnp.where(expert < 3 * EXPERTS, expert % EXPERTS, -1)
    gate = jnp.sum(jnp.where(own_idx[:, :, None] == expert[None, None, :], gates[:, :, None], 0.0), axis=1)
    head_rows = attention(query, keys, values)
    h = head_rows.reshape(4, 4, 32, 256)
    h = gray(gray(h, 0), 1).reshape(2, 2, 2, 2, 2, 16, 256)

    member = jnp.any(route_idx == exp_pos, axis=1)
    count = jnp.sum(member.astype(F32))
    member = gathered_order(member.astype(BF)).reshape(128, 16)
    before = (jnp.arange(16)[:, None] < jnp.arange(16)[None, :]).astype(BF)
    rank = jnp.dot(member, before, preferred_element_type=F32)
    rank = jnp.where(member > 0, rank, -1.0).astype(jnp.int32).reshape(8, 1, 256)
    slot = jnp.arange(128, dtype=jnp.int32)[None, :, None]
    token = jnp.arange(256, dtype=jnp.int32)[None, None, :]
    sel = jnp.logical_and(slot // 8 == token // 16, slot % 8 == rank)
    exp = jnp.transpose(sel, (0, 2, 1)).astype(BF)
    sel = sel.astype(BF)

    mixed, attn_out, gram = fused(
        h, out_weight, resid, post_gain.reshape(1, D), gate, sel, exp, w_gate[0], w_up[0], w_down[0]
    )
    return (mixed, attn_out, (gram / count)[None])


def solution(mesh):
    placed = (
        P(("ctx", "exp"), None),
        P("ctx", "exp"),
        P("ctx", None),
        P("ctx", None),
        P("exp", None),
        P(),
        P(),
        P(("ctx", "exp"), None),
        P("exp", None, "ctx"),
        P("exp", None, "ctx"),
        P("exp", "ctx", None),
    )
    return jax.shard_map(
        local,
        mesh=mesh,
        in_specs=placed,
        out_specs=(P(("ctx", "exp"), None), P(("ctx", "exp"), None), P("exp", "ctx", None)),
        check_vma=False,
    )
```

time: 475 us -> 225 us (0.47)
  waiting for transfers between devices: 359 us -> 17.5 us
  Pallas kernels: 0 us -> 165 us
  blocking collectives: 42.4 us -> 0 us
  matrix products: 36 us -> 10.8 us
  starting transfers between devices: 7.38 us -> 0.04 us
    reduce_scatter x2 -> x0, waiting for transfers between devices: 223 us -> none  [the longest x1 146 us: local(): lax.psum_scatter(jnp.dot(rows, out_weight, preferred_element_type=jnp.flo...]
    pallas_call x0 -> x1, Pallas kernels: none -> 165 us  [fused(): pl.pallas_call(kernel, out_shape=(jax.ShapeDtypeStruct((16, D), BF), jax....]
    all_gather x2 -> x1, waiting for transfers between devices: 135 us -> 17.5 us  [attention(): both = lax.all_gather(both, 'ctx', axis=0, tiled=True)]
    dot_general x9 -> x2, matrix products: 36 us -> 3.13 us  [the longest x1 2.94 us: attention(): jnp.einsum('hqk,kd->qhd', weights, v_piece, preferred_element_type=F32)]
    all_to_all x1 -> x0, blocking collectives: 22.2 us -> none  [local(): lax.all_to_all(send, 'exp', split_axis=0, concat_axis=0, tiled=True)]
    all_gather x2 -> x0, blocking collectives: 20.2 us -> none  [the longest x1 11.4 us: local(): v_piece = lax.all_gather(value_part, 'ctx', axis=0, tiled=True)]
    sub x0 -> x1, matrix products: none -> 7.63 us  [attention(): scores - peak[:, :, None]]
    all_to_all x1 -> x0, starting transfers between devices: 7.04 us -> none  [local(): lax.all_to_all(outgoing, 'exp', split_axis=0, concat_axis=0, tiled=True)]
  transfers between devices with their start and end apart: 5 -> 1, of which waited for: 4 -> 1; matrix products, arithmetic and copies ran while one was open for 1% -> 4% of each run, Pallas kernels for 0% -> 0%
where the time goes in v1:
time: 225 us; the launch traced here: 224 us
  Pallas kernels  165 us (73%)
  waiting for transfers between devices  17.5 us (8%)
  between operations  14.3 us (6%)
  other arithmetic  10.9 us (5%)
  matrix products  10.8 us (5%)
  local copies, waits for them, and re-layouts  5.68 us (3%)
    pallas_call x1, Pallas kernels, fused(): pl.pallas_call(kernel, out_shape=(jax.ShapeDtypeStruct((16, D), BF), jax....  165 us
    all_gather x1, waiting for transfers between devices, attention(): both = lax.all_gather(both, 'ctx', axis=0, tiled=True)  17.5 us
    sub x1, matrix products, attention(): scores - peak[:, :, None]  7.63 us
  transfers between devices with their start and end apart: 1, of which 1 were waited for; matrix products, arithmetic and copies ran while one was open for 4% of the time, Pallas kernels for 0%

profile of v1, /device:TPU:1, one launch (start us, length us, event | category | flops | bytes accessed | tf_op | source)
XLA Modules:
  0.0 224.3 jit_solution(5529430904492095709)
XLA Ops:
  7.2 0.0 copy-start
  7.2 0.0 all-gather.2.cloned.1.call-start
  7.2 1.0 constant_dynamic-slice_fusion.1
  8.2 0.7 pad_maximum_fusion
  9.0 0.0 all-gather.2.cloned.1.call-update
  9.0 0.9 compare_reduce_fusion
  9.9 0.1 reshape.193
  10.0 0.1 slice.101
  10.1 0.1 slice.103
  10.2 0.1 slice.105
  10.3 0.1 slice.107
  10.6 0.7 convert_reduce_fusion.1
  11.2 0.8 constant_dynamic-slice_fusion
  12.0 0.1 reshape_reshape.4
  12.1 0.1 copy.62
  12.2 0.2 fusion.7
  12.4 0.8 copy.57
  13.2 0.1 copy.56
  13.2 0.1 copy.63
  13.3 0.1 eq.79
  13.4 0.7 select_reduce_fusion.gate_ref
  14.1 0.1 broadcast_compare_fusion.1
  14.2 0.1 broadcast_compare_fusion
  14.3 1.0 and_convert_fusion.1.sel_ref
  15.3 1.1 and_convert_fusion.exp_ref
  16.5 0.8 iota_compare_fusion
  17.3 17.5 %all-gather.2.cloned.1.call-done = bf16[2048,256]{1,0:T(8,128)(2,1)} async-done(((bf16[512,256]{1,0:T(8,128)(2,1)}), bf16[2048,256]{1,0:T(8,128)(2,1)}) %all-gather.2.cloned.1.call-update) | async-done | bytes 1048592 | tf_op jit(solution)/shard_map/all_gather | solution.py:404
  34.8 0.0 copy-done
  34.8 0.0 copy-start.3
  34.8 7.6 %convert_reduce_fusion = (f32[2,512]{1,0:T(2,128)S(1)}, bf16[2,512,2048]{1,2,0:T(8,128)(2,1)}) fusion(pred[512,2048]{0,1:T(8,128)(4,1)S(1)} %iota_compare_fusion, bf16[2048,256]{1,0:T(8,128)(2,1)} %all-gather.2.cloned.1.call-done, bf16[512,256]{1,0:T(8,128)(2,1)S(1)} %copy-done), kind=kOutput, calls=%fused_computation.2 | convolution fusion | flops 551553024 | bytes 7081984 | tf_op jit(solution)/shard_map/sub | solution.py:413
  42.4 0.0 copy-done.3
  42.5 2.9 %fusion.6 = bf16[512,2,128]{0,2,1:T(8,128)(2,1)S(1)} fusion(bf16[2,512,2048]{1,2,0:T(8,128)(2,1)} %get-tuple-element.24, bf16[2048,256]{1,0:T(8,128)(2,1)S(1)} %copy-done.3, f32[512,2]{0,1:T(2,128)S(1)} %bitcast.68), kind=kOutput, calls=%fused_computation.12 | convolution fusion | flops 537133056 | bytes 4984832 | tf_op jit(solution)/shard_map/hqk,kd->qhd/dot_general | solution.py:415
  45.4 0.1 copy.52
  45.6 0.1 copy.53
  45.8 0.1 copy.54
  46.0 0.1 copy.55
  46.3 0.7 pad_maximum_fusion.1
  47.0 165.2 %layer.1 = (bf16[16,4096]{1,0:T(8,128)(2,1)}, f32[16,4096]{1,0:T(8,128)}, f32[384,1536]{1,0:T(8,128)}) custom-call(bf16[2,2,2,2,2,16,256]{6,5,4,3,2,1,0:T(8,128)(2,1)} %bitcast.65, bf16[256,4096]{1,0:T(8,128)(2,1)} %ow_ref.1, bf16[16,4096]{1,0:T(8,128)(2,1)} %resid_ref.1, f32[1,4096]{1,0:T(1,128)} %bitcast.67, f32[16,128]{1,0:T(8,128)} %select_reduce_fusion.gate_ref, ...), custom_call_target="tpu_custom_call" | custom-call | tf_op jit(solution)/shard_map/layer/pallas_call | solution.py:360
  212.2 0.0 copy-start.2
  212.2 0.0 copy-start.1
  212.2 3.9 %divide_bitcast_fusion = f32[1,384,1536]{2,1,0:T(8,128)} fusion(f32[384,1536]{1,0:T(8,128)} %get-tuple-element.8, f32[]{:T(128)} %convert_reduce_fusion.1), kind=kLoop, calls=%fused_computation.9 | loop fusion | flops 589824 | bytes 4718596 | tf_op jit(solution)/shard_map/broadcast_in_dim | solution.py:447
  216.1 0.0 copy-done.2
  216.1 0.7 copy.92
  216.8 0.0 copy-done.1
  216.8 0.7 copy.93
  (31 shorter events, 0.5 us)
Async XLA Ops:
  7.2 27.7 %copy-start = (bf16[512,256]{1,0:T(8,128)(2,1)S(1)}, bf16[512,256]{1,0:T(8,128)(2,1)}, u32[]{:S(2)}) copy-start(bf16[512,256]{1,0:T(8,128)(2,1)} %param.12) | copy-start | bytes 786436
  7.2 27.6 %all-gather.2.cloned.1.call-start = ((), (), s32[]{:S(2)}) async-start(), calls=%async_computation | async-start | bytes 1310720 | tf_op jit(solution)/shard_map/all_gather | solution.py:404
  34.8 7.6 %copy-start.3 = (bf16[2048,256]{1,0:T(8,128)(2,1)S(1)}, bf16[2048,256]{1,0:T(8,128)(2,1)}, u32[]{:S(2)}) copy-start(bf16[2048,256]{1,0:T(8,128)(2,1)} %all-gather.2.cloned.1.call-done) | copy-start | bytes 3145732
  212.2 3.9 %copy-start.2 = (bf16[16,4096]{1,0:T(8,128)(2,1)S(1)}, bf16[16,4096]{1,0:T(8,128)(2,1)}, u32[]{:S(2)}) copy-start(bf16[16,4096]{1,0:T(8,128)(2,1)} %get-tuple-element.32) | copy-start | bytes 393220
  212.2 4.6 %copy-start.1 = (f32[16,4096]{1,0:T(8,128)S(1)}, f32[16,4096]{1,0:T(8,128)}, u32[]{:S(2)}) copy-start(f32[16,4096]{1,0:T(8,128)} %get-tuple-element.33) | copy-start | bytes 786436
Sparse Core Ops, SparseCore 0:
  10.3 24.5 all-gather.1

commit v2 on v1

--- a/solution.py
+++ b/solution.py
@@ -8,9 +8,7 @@
 from jax.experimental.pallas import tpu as pltpu
 from jax.sharding import PartitionSpec as P
 
-QUERY_HEADS = 64
 EXPERTS = 32
-KEY_VALUE_HEADS = 4
 HEAD_SIZE = 128
 D = 4096
 FF = 1536
@@ -37,11 +35,13 @@
 
 
 def kernel(
-    h_ref, ow_ref, resid_ref, gain_ref, gate_ref, sel_ref, exp_ref, wg_ref, wu_ref, wd_ref,
+    q_ref, ow_ref, resid_ref, gain_ref, gate_ref, rank_ref, keys_ref, values_ref, wg_ref, wu_ref, wd_ref,
     mixed_ref, attn_ref, gram_ref,
+    kv, top_s, sum_s, acc_s, h_ref, sel_ref,
     p1, r10, r11, r12, r13, r14, norm, stream, csh, x0, x1, x2, x3, x4, x5,
     wgk, wuk, wgs, wus, wdq, xs, psend, precv, hall, p2, r20, r21, r22, r23, r24, fsend, frecv,
-    s1s, s1r, wss, wsr, lsem, ccs, ccr, ags, agr, pss, psr, hss, hsr, s2s, s2r, fss, fsr,
+    kvl, kvs, kvr,
+    s1s, s1r, wss, wsr, lsem, ccs, ccr, ags, agr, pss, psr, hss, hsr, has, har, s2s, s2r, fss, fsr,
 ):
     c = lax.axis_index("ctx")
     e = lax.axis_index("exp")
@@ -77,6 +77,81 @@
             src_ref=src, dst_ref=dst, send_sem=ss, recv_sem=rs, device_id=to, device_id_type=MESH
         )
 
+    head_cols = pl.ds(pl.multiple_of(x * HEAD_SIZE, HEAD_SIZE), HEAD_SIZE)
+    kv_src = (keys_ref.at[:, head_cols], values_ref.at[:, head_cols])
+
+    def kv_copy(i, to, cc, j):
+        return remote(kv_src[j], kv.at[cc, j], kvs.at[i, j], kvr.at[cc, j], to)
+
+    for j in range(2):
+
+        @pl.when(zh == 0)
+        def _():
+            kv_copy(1, far, c, j).start()
+            kv_copy(2, farsib, c, j).start()
+
+    for j in range(2):
+
+        @pl.when(k == 0)
+        def _():
+            kv_copy(0, sib, c, j).start()
+
+        pltpu.make_async_copy(kv_src[j], kv.at[c, j], kvl.at[j]).start()
+
+    slot = lax.broadcasted_iota(jnp.int32, (128, 256), 0)
+    token = lax.broadcasted_iota(jnp.int32, (128, 256), 1)
+    place = jnp.where(slot // 8 == token // 16, slot % 8, -2)
+
+    def pick_slots(g):
+        sel_ref[g] = jnp.where(place == rank_ref[g], 1.0, 0.0).astype(BF)
+
+    pl.loop(0, 8)(pick_slots)
+    top_s[...] = jnp.full((4, 256, 1), -1e30, F32)
+    sum_s[...] = jnp.zeros((4, 256, 1), F32)
+    acc_s[...] = jnp.zeros((4, 256, HEAD_SIZE), F32)
+    for j in range(2):
+        pltpu.make_async_copy(kv_src[j], kv.at[c, j], kvl.at[j]).wait()
+    q_place = lax.rem(lax.broadcasted_iota(jnp.int32, (256, 512), 0), 128)
+    k_place = lax.broadcasted_iota(jnp.int32, (256, 512), 1)
+    scale = 1.0 / math.sqrt(HEAD_SIZE)
+
+    def key_block(i):
+        cc = c - i
+
+        @pl.when(i > 0)
+        def _():
+            for j in range(2):
+                kv_copy(0, sib, cc, j).wait_recv()
+
+        def tile(t):
+            rows = pl.ds(pl.multiple_of(t * 128, 128), 128)
+            q = jnp.concatenate([q_ref[rows, :HEAD_SIZE], q_ref[rows, HEAD_SIZE:]], axis=0)
+            scores = lax.dot_general(q, kv[cc, 0], (((1,), (1,)), ((), ())), preferred_element_type=F32) * scale
+            allowed = q_place + (t * 128 + i * 512) >= k_place
+            scores = jnp.where(allowed, scores, -1e30)
+            old = top_s[t]
+            new = jnp.maximum(old, jnp.max(scores, axis=1, keepdims=True))
+            w = jnp.where(allowed, jnp.exp(scores - new), 0.0).astype(BF)
+            fade = jnp.exp(old - new)
+            top_s[t] = new
+            sum_s[t] = sum_s[t] * fade + jnp.sum(w.astype(F32), axis=1, keepdims=True)
+            acc_s[t] = acc_s[t] * fade + jnp.dot(w, kv[cc, 1], preferred_element_type=F32)
+
+        pl.loop(0, 4)(tile)
+
+    pl.loop(0, c + 1)(key_block)
+
+    def head_tile(t):
+        out = (acc_s[t] / sum_s[t]).astype(BF)
+        b1 = t // 2
+        b0 = (b1 + t % 2) % 2
+        for hd in range(2):
+            for yy in range(4):
+                at = hd * 128 + yy * 32
+                h_ref[b1, b0, yy // 2, (yy // 2 + yy) % 2, :, :, hd * 128 : hd * 128 + 128] = out[at : at + 32].reshape(2, 16, 128)
+
+    pl.loop(0, 4)(head_tile)
+
     def rs_index(f, s, bit):
         order = RS_ORDER[f]
         idx = [FULL] * 5
@@ -91,21 +166,26 @@
             buf.at[(f,) + rs_index(f, s, 1 - own5[d])], recv[s].at[f], ss.at[f, s], rs.at[f, s], rs_peer[d]
         )
 
-    def rs_add(buf, recv, f, s):
+    def rs_add(buf, recv, f, s, bit):
         order = RS_ORDER[f]
-        left = sorted(order[s + 1 :])
+        step = order[s + 1]
+        left = sorted(order[s + 2 :])
         n = len(left)
 
         def one(i):
-            bits = block_bits(i, n)
+            bits = dict(zip(left, block_bits(i, n)))
+            bits[step] = bit
             idx = list(own5)
-            for d, b in zip(left, bits):
-                idx[d] = b
+            for d in bits:
+                idx[d] = bits[d]
             idx = (f,) + tuple(idx)
-            got = recv[s][(f,) + tuple(bits)]
+            got = recv[s][(f,) + tuple(bits[d] for d in sorted(bits))]
             buf[idx] = (buf[idx].astype(F32) + got.astype(F32)).astype(BF)
 
-        pl.loop(0, 2**n)(one)
+        if n:
+            pl.loop(0, 2**n)(one)
+        else:
+            one(0)
 
     recv1 = (r10, r11, r12, r13, r14)
     recv2 = (r20, r21, r22, r23, r24)
@@ -149,22 +229,37 @@
 
     for f in range(4):
         project(f, own5[RS_ORDER[f][0]])
-
-    def finish_rs(buf, recv, ss, rs, first):
-        last = list(first)
+    for j in range(2):
+
+        @pl.when(zh == 0)
+        def _():
+            kv_copy(1, far, c, j).wait_send()
+            kv_copy(2, farsib, c, j).wait_send()
+
+        @pl.when(k == 0)
+        def _():
+            kv_copy(0, sib, c, j).wait_send()
+
+    def finish_rs(buf, recv, ss, rs, wait_first):
+        last = [None] * 4
         for s in range(4):
             for f in range(4):
-                last[f].wait()
-                rs_add(buf, recv, f, s)
+                if s == 0:
+                    wait_first(f)
+                else:
+                    last[f].wait()
+                d = RS_ORDER[f][s + 1]
+                rs_add(buf, recv, f, s, 1 - own5[d])
                 last[f] = rs_copy(buf, recv, ss, rs, f, s + 1)
                 last[f].start()
+                rs_add(buf, recv, f, s, own5[d])
         out = []
         for f in range(4):
             last[f].wait()
             out.append(buf[(f,) + own5].astype(F32) + recv[4][f].astype(F32))
         return out
 
-    parts = finish_rs(p1, recv1, s1s, s1r, first)
+    parts = finish_rs(p1, recv1, s1s, s1r, lambda f: first[f].wait())
 
     squares = jnp.zeros((16, 1), F32)
     for f in range(4):
@@ -202,107 +297,158 @@
         xf[f][own6 + (sib_tok, slice(0, USED[f]))] = csh[:, OFFS[f] : OFFS[f] + USED[f]]
     x4[own6 + (sib_tok, slice(256, 384))] = csh[:, HALF:]
 
-    def ag_copy(f, s):
-        done = [CYCLE[(f + t) % 6] for t in range(s)]
-        d = CYCLE[(f + s) % 6]
-        idx = tuple(FULL if j in done else own6[j] for j in range(6))
-        return remote(xf[f].at[idx], xf[f].at[idx], ags.at[f, s], agr.at[f, s], ag_peer[d])
-
-    last = []
-    for f in range(6):
-        cp = ag_copy(f, 0)
-        cp.start()
-        last.append(cp)
-    for s in range(1, 6):
+    def ag_copy(f, s, j):
+        idx = list(own6)
+        for t in range(j):
+            idx[CYCLE[(f + t) % 6]] = FULL
+        if j >= 0:
+            d = CYCLE[(f + j) % 6]
+            idx[d] = 1 - own6[d]
+        part = xf[f].at[tuple(idx)]
+        return remote(part, part, ags.at[f, s, j + 1], agr.at[f, s, j + 1], ag_peer[CYCLE[(f + s) % 6]])
+
+    for s in range(6):
         for f in range(6):
-            last[f].wait()
-            last[f] = ag_copy(f, s)
-            last[f].start()
-    for f in range(6):
-        last[f].wait()
-
-    def select(g):
-        b = block_bits(g, 3)
-        pick = sel_ref[g]
-        rows = pl.ds(pl.multiple_of(g * 128, 128), 128)
+            ag_copy(f, s, -1).start()
+    for s in range(6):
         for f in range(6):
-            block = xf[f][tuple(b)].reshape(256, WIDTHS[f])[:, : USED[f]]
-            xs[rows, OFFS[f] : OFFS[f] + USED[f]] = jnp.dot(pick, block, preferred_element_type=F32).astype(BF)
-
-    pl.loop(0, 8)(select)
+            for j in range(-1, s):
+                ag_copy(f, s, j).wait_recv()
+            for t in range(s + 1, 6):
+                ag_copy(f, t, s).start()
+    for s in range(6):
+        for f in range(6):
+            for j in range(-1, s):
+                ag_copy(f, s, j).wait_send()
+
     for cp in weight_copies + local_copies:
         cp.wait()
 
+    def chunk_bits(i):
+        return (1 - own5[0] + i // 2) % 2, (1 - own5[1] + i % 2) % 2
+
+    def chunk(i):
+        b1, b0 = chunk_bits(i)
+        return b1 * 2 + b0
+
+    def chunk_rows(m):
+        return pl.ds(pl.multiple_of(m * 256, 256), 256)
+
+    def select(m):
+        for g in range(2):
+            pick = sel_ref[m * 2 + g]
+            rows = pl.ds(pl.multiple_of(m * 256 + g * 128, 128), 128)
+            for f in range(6):
+                block = xf[f][m // 2, m % 2, g].reshape(256, WIDTHS[f])[:, : USED[f]]
+                xs[rows, OFFS[f] : OFFS[f] + USED[f]] = jnp.dot(pick, block, preferred_element_type=F32).astype(BF)
+
     def partial_copy(m):
         return remote(psend.at[m], precv.at[m], pss.at[m], psr.at[m], sib)
 
     def other_units(m):
-        a = xs[pl.ds(pl.multiple_of(m * 256, 256), 256), :]
+        a = xs[chunk_rows(m), :]
         psend[m, :, :FFS] = jnp.dot(a, wgs[...], preferred_element_type=F32).astype(BF)
         psend[m, :, FFS:] = jnp.dot(a, wus[...], preferred_element_type=F32).astype(BF)
         partial_copy(m).start()
 
-    pl.loop(0, 4)(other_units)
-
     def hidden_cols(cc):
         return pl.ds(pl.multiple_of(cc * FFS, 128), FFS)
 
     def hidden_copy(m, cc, kind, to):
-        part = hall.at[pl.ds(pl.multiple_of(m * 256, 256), 256), hidden_cols(cc)]
+        part = hall.at[chunk_rows(m), hidden_cols(cc)]
         return remote(part, part, hss.at[kind, m], hsr.at[kind, m], to)
 
     def own_units(m):
-        rows = pl.ds(pl.multiple_of(m * 256, 256), 256)
-        a = xs[rows, :]
+        a = xs[chunk_rows(m), :]
         gate = jnp.dot(a, wgk[...], preferred_element_type=F32)
         upper = jnp.dot(a, wuk[...], preferred_element_type=F32)
         partial_copy(m).wait()
         gate = gate + precv[m, :, :FFS].astype(F32)
         upper = upper + precv[m, :, FFS:].astype(F32)
-        hall[rows, hidden_cols(c)] = (gate / (1.0 + jnp.exp(-gate)) * upper).astype(BF)
+        hall[chunk_rows(m), hidden_cols(c)] = (gate / (1.0 + jnp.exp(-gate)) * upper).astype(BF)
         hidden_copy(m, c, 0, far).start()
         hidden_copy(m, c, 1, sib).start()
 
-    pl.loop(0, 4)(own_units)
+    def units(i):
+        @pl.when(i < 4)
+        def _():
+            m = chunk(i)
+            select(m)
+            other_units(m)
+
+        @pl.when(i > 0)
+        def _():
+            own_units(chunk(i - 1))
+
+    pl.loop(0, 5)(units)
     far_c = (1 - zh) * 2 + k
 
-    def forward(m):
-        hidden_copy(m, c, 0, far).wait()
-        hidden_copy(m, far_c, 2, sib).start()
-
-    pl.loop(0, 4)(forward)
-
-    def down(m):
+    def half_copy(f, b1, b0):
+        if f == 0:
+            src, dst, sem = p2.at[0, b1, b0], r20.at[0, b0], b0
+        elif f == 2:
+            src, dst, sem = p2.at[2, b1, b0], r20.at[2, b1], b1
+        elif f == 1:
+            src, dst, sem = p2.at[1, b1, b0, 1 - own5[2]], r20.at[1, b1, b0], b1 * 2 + b0
+        else:
+            src, dst, sem = p2.at[3, b1, b0, :, 1 - own5[3]], r20.at[3, b1, b0], b1 * 2 + b0
+        return remote(src, dst, has.at[f, sem], har.at[f, sem], rs_peer[RS_ORDER[f][0]])
+
+    lane = lax.broadcasted_iota(jnp.int32, (256, 128), 1)
+    my_lanes = jnp.logical_or(lane == e, jnp.logical_or(lane == e + EXPERTS, lane == e + 2 * EXPERTS))
+
+    def down(i):
+        b1, b0 = chunk_bits(i)
+        m = b1 * 2 + b0
         hidden_copy(m, c, 1, sib).wait()
         hidden_copy(m, far_c, 2, sib).wait()
-        rows = pl.ds(pl.multiple_of(m * 256, 256), 256)
-        a = hall[rows, :]
-        b1, b0 = m // 2, m % 2
-        lane = lax.broadcasted_iota(jnp.int32, (256, 128), 1)
-        mine = jnp.logical_or(lane == e, jnp.logical_or(lane == e + EXPERTS, lane == e + 2 * EXPERTS))
+        a = hall[chunk_rows(m), :]
         weights = []
         for g in range(2):
             block = x4[b1, b0, g].reshape(256, 384)[:, 256:].astype(F32)
-            weights.append(jnp.sum(jnp.where(mine, block, 0.0), axis=1, keepdims=True))
+            weights.append(jnp.sum(jnp.where(my_lanes, block, 0.0), axis=1, keepdims=True))
         for f in range(4):
             cols = slice(f * 256, f * 256 + 256)
             out = jnp.dot(a, wdq[:, cols], preferred_element_type=F32).astype(BF)
             for g in range(2):
-                tok = jnp.dot(exp_ref[m * 2 + g], out[g * 128 : g * 128 + 128], preferred_element_type=F32)
+                tok = lax.dot_general(
+                    sel_ref[m * 2 + g], out[g * 128 : g * 128 + 128], (((0,), (0,)), ((), ())),
+                    preferred_element_type=F32,
+                )
                 tok = (tok * weights[g]).astype(BF)
                 for yb in range(2):
                     for j in range(4):
                         zlo, zhi = ZMAP[j]
                         at = (yb * 4 + j) * 32
                         p2[f, b1, b0, g, yb, zlo, zhi * 32 : zhi * 32 + 32, :] = tok[at : at + 32]
-
-    pl.loop(0, 4)(down)
-
-    first = []
-    for f in range(4):
-        cp = rs_copy(p2, recv2, s2s, s2r, f, 0)
-        cp.start()
-        first.append(cp)
+            if f == 0:
+                pl.when(i < 2)(lambda: half_copy(0, b1, b0).start())
+            elif f == 2:
+                pl.when(i % 2 == 0)(lambda: half_copy(2, b1, b0).start())
+            else:
+                half_copy(f, b1, b0).start()
+
+    def spread(i):
+        @pl.when(i < 4)
+        def _():
+            m = chunk(i)
+            hidden_copy(m, c, 0, far).wait()
+            hidden_copy(m, far_c, 2, sib).start()
+
+        @pl.when(i > 0)
+        def _():
+            down(i - 1)
+
+    pl.loop(0, 5)(spread)
+
+    def wait_half(f):
+        for b in range(2 if f % 2 == 0 else 4):
+            if f == 0:
+                half_copy(0, 1 - own5[0], b).wait()
+            elif f == 2:
+                half_copy(2, b, 1 - own5[1]).wait()
+            else:
+                half_copy(f, b // 2, b % 2).wait()
 
     def gram(j):
         cols = pl.ds(pl.multiple_of(j * 256, 256), 256)
@@ -312,7 +458,7 @@
 
     pl.loop(0, 6)(gram)
 
-    parts = finish_rs(p2, recv2, s2s, s2r, first)
+    parts = finish_rs(p2, recv2, s2s, s2r, wait_half)
     for f in range(4):
         cols = slice(f * 256, f * 256 + 256)
         fsend[:, :, cols] = parts[f].astype(BF).reshape(4, 16, 256)
@@ -331,7 +477,7 @@
         mixed_ref[:, cols] = (stream[:, cols].astype(F32) + frecv[cc].astype(F32)).astype(BF)
 
 
-def fused(h, ow, resid, gain, gate, sel, exp, wg, wu, wd):
+def fused(q, ow, resid, gain, gate, rank, keys, values, wg, wu, wd):
     dma = pltpu.SemaphoreType.DMA
     vm = pl.BlockSpec(memory_space=pltpu.VMEM)
     hbm = pl.BlockSpec(memory_space=pl.ANY)
@@ -344,7 +490,9 @@
         return out
 
     scratch = (
-        rs_scratch(16, 1024)
+        [pltpu.VMEM((4, 2, 512, HEAD_SIZE), BF), pltpu.VMEM((4, 256, 1), F32), pltpu.VMEM((4, 256, 1), F32)]
+        + [pltpu.VMEM((4, 256, HEAD_SIZE), F32), pltpu.VMEM((2,) * 5 + (16, 256), BF), pltpu.VMEM((8, 128, 256), BF)]
+        + rs_scratch(16, 1024)
         + [pltpu.VMEM((2, 16, WIDE), BF), pltpu.VMEM((16, D), BF), pltpu.VMEM((16, WIDE), BF)]
         + [pltpu.VMEM(two + (32, w), BF) for w in WIDTHS]
         + [pltpu.VMEM((HALF, FFS), BF)] * 4
@@ -353,9 +501,10 @@
         + [pltpu.VMEM((1024, FF), BF)]
         + rs_scratch(64, 256)
         + [pltpu.VMEM((4, 16, QUART), BF)] * 2
+        + [dma((2,)), dma((3, 2)), dma((4, 2))]
         + [dma((4, 5)), dma((4, 5)), dma((5,)), dma((5,)), dma((3,)), dma((1,)), dma((1,))]
-        + [dma((6, 6)), dma((6, 6)), dma((4,)), dma((4,)), dma((3, 4)), dma((3, 4))]
-        + [dma((4, 5)), dma((4, 5)), dma((3,)), dma((3,))]
+        + [dma((6, 6, 6)), dma((6, 6, 6)), dma((4,)), dma((4,)), dma((3, 4)), dma((3, 4))]
+        + [dma((4, 4)), dma((4, 4)), dma((4, 5)), dma((4, 5)), dma((3,)), dma((3,))]
     )
     return pl.pallas_call(
         kernel,
@@ -364,14 +513,14 @@
             jax.ShapeDtypeStruct((16, D), F32),
             jax.ShapeDtypeStruct((FFS, FF), F32),
         ),
-        in_specs=[vm] * 7 + [hbm] * 3,
+        in_specs=[vm] * 6 + [hbm] * 5,
         out_specs=(vm, vm, vm),
         scratch_shapes=scratch,
         compiler_params=pltpu.CompilerParams(
             collective_id=0, has_side_effects=True, vmem_limit_bytes=62 * 2**20
         ),
         name="layer",
-    )(h, ow, resid, gain, gate, sel, exp, wg, wu, wd)
+    )(q, ow, resid, gain, gate, rank, keys, values, wg, wu, wd)
 
 
 def gray(a, axis):
@@ -390,32 +539,6 @@
     return a.reshape((2048,) + rest)
 
 
-def attention(query, keys, values):
-    ctx_pos = lax.axis_index("ctx")
-    exp_pos = lax.axis_index("exp")
-    span = query.shape[0]
-    heads = query.shape[1] // HEAD_SIZE
-    head_group = QUERY_HEADS // KEY_VALUE_HEADS
-    scale = 1.0 / math.sqrt(HEAD_SIZE)
-    kv_head = exp_pos * heads // head_group
-    key_part = lax.dynamic_slice_in_dim(keys, kv_head * HEAD_SIZE, HEAD_SIZE, 1)
-    value_part = lax.dynamic_slice_in_dim(values, kv_head * HEAD_SIZE, HEAD_SIZE, 1)
-    both = jnp.concatenate([key_part, value_part], axis=1)
-    both = lax.all_gather(both, "ctx", axis=0, tiled=True)
-    k_piece, v_piece = both[:, :HEAD_SIZE], both[:, HEAD_SIZE:]
-    q_heads = query.reshape(span, heads, HEAD_SIZE)
-    q_place = ctx_pos * span + jnp.arange(span, dtype=jnp.int32)
-    scores = jnp.einsum("qhd,kd->hqk", q_heads, k_piece, preferred_element_type=F32) * scale
-    k_place = jnp.arange(k_piece.shape[0], dtype=jnp.int32)
-    allowed = (q_place[:, None] >= k_place[None, :])[None]
-    scores = jnp.where(allowed, scores, -1e30)
-    peak = jnp.max(scores, axis=2)
-    weights = jnp.where(allowed, jnp.exp(scores - peak[:, :, None]), 0.0).astype(BF)
-    total = jnp.sum(weights.astype(F32), axis=2)
-    accum = jnp.einsum("hqk,kd->qhd", weights, v_piece, preferred_element_type=F32)
-    return (accum / total.T[:, :, None]).astype(BF).reshape(span, heads * HEAD_SIZE)
-
-
 def local(
     resid, query, keys, values, out_weight, post_gain, route_idx, gates, w_gate, w_up, w_down
 ):
@@ -425,24 +548,14 @@
     expert = jnp.arange(128, dtype=jnp.int32)
     expert = jnp.where(expert < 3 * EXPERTS, expert % EXPERTS, -1)
     gate = jnp.sum(jnp.where(own_idx[:, :, None] == expert[None, None, :], gates[:, :, None], 0.0), axis=1)
-    head_rows = attention(query, keys, values)
-    h = head_rows.reshape(4, 4, 32, 256)
-    h = gray(gray(h, 0), 1).reshape(2, 2, 2, 2, 2, 16, 256)
-
     member = jnp.any(route_idx == exp_pos, axis=1)
     count = jnp.sum(member.astype(F32))
     member = gathered_order(member.astype(BF)).reshape(128, 16)
     before = (jnp.arange(16)[:, None] < jnp.arange(16)[None, :]).astype(BF)
     rank = jnp.dot(member, before, preferred_element_type=F32)
     rank = jnp.where(member > 0, rank, -1.0).astype(jnp.int32).reshape(8, 1, 256)
-    slot = jnp.arange(128, dtype=jnp.int32)[None, :, None]
-    token = jnp.arange(256, dtype=jnp.int32)[None, None, :]
-    sel = jnp.logical_and(slot // 8 == token // 16, slot % 8 == rank)
-    exp = jnp.transpose(sel, (0, 2, 1)).astype(BF)
-    sel = sel.astype(BF)
-
     mixed, attn_out, gram = fused(
-        h, out_weight, resid, post_gain.reshape(1, D), gate, sel, exp, w_gate[0], w_up[0], w_down[0]
+        query, out_weight, resid, post_gain.reshape(1, D), gate, rank, keys, values, w_gate[0], w_up[0], w_down[0]
     )
     return (mixed, attn_out, (gram / count)[None])
 

time: 225 us -> 183 us (0.81)
  waiting for transfers between devices: 17.5 us -> 0 us
  between operations: 14.3 us -> 0.76 us
  matrix products: 10.8 us -> 0.19 us
  Pallas kernels: 165 us -> 171 us
  other arithmetic: 10.9 us -> 6.29 us
    all_gather x1 -> x0, waiting for transfers between devices: 17.5 us -> none  [attention(): both = lax.all_gather(both, 'ctx', axis=0, tiled=True)]
    sub x1 -> x0, matrix products: 7.63 us -> none  [attention(): scores - peak[:, :, None]]
    pallas_call x1, Pallas kernels: 165 us -> 171 us  [fused(): pl.pallas_call(kernel, out_shape=(jax.ShapeDtypeStruct((16, D), BF), jax....]
    dot_general x1 -> x0, matrix products: 2.94 us -> none  [attention(): jnp.einsum('hqk,kd->qhd', weights, v_piece, preferred_element_type=F32)]
  transfers between devices with their start and end apart: 1 -> 0, of which waited for: 1 -> 0; matrix products, arithmetic and copies ran while one was open for 4% -> 0% of each run, Pallas kernels for 0% -> 0%
where the time goes in v2:
time: 183 us; the launch traced here: 182 us
  Pallas kernels  171 us (93%)
  other arithmetic  6.29 us (3%)
  local copies, waits for them, and re-layouts  4.49 us (2%)
    pallas_call x1, Pallas kernels, fused(): pl.pallas_call(kernel, out_shape=(jax.ShapeDtypeStruct((16, D), BF), jax....  171 us
    broadcast_in_dim x1, other arithmetic, local(): return (mixed, attn_out, (gram / count)[None])  3.97 us

profile of v2, /device:TPU:1, one launch (start us, length us, event | category | flops | bytes accessed | tf_op | source)
XLA Modules:
  0.0 182.4 jit_solution(7249028859998508043)
XLA Ops:
  0.6 0.9 compare_reduce_fusion
  1.5 0.7 convert_reduce_fusion
  2.2 0.8 constant_dynamic-slice_fusion
  3.0 0.1 copy.31
  3.0 0.8 copy.32
  3.8 0.7 select_reduce_fusion.gate_ref
  4.5 0.1 reshape.37
  4.6 0.1 slice.53
  4.7 0.1 slice.51
  4.8 0.1 slice.49
  4.9 0.1 slice.47
  5.2 0.1 reshape_reshape.3
  5.3 0.1 copy.37
  5.3 0.2 fusion
  5.5 0.1 copy.38
  5.7 0.7 reshape.38.rank_ref
  6.4 170.7 %layer.1 = (bf16[16,4096]{1,0:T(8,128)(2,1)}, f32[16,4096]{1,0:T(8,128)}, f32[384,1536]{1,0:T(8,128)}) custom-call(bf16[512,256]{1,0:T(8,128)(2,1)} %q_ref.1, bf16[256,4096]{1,0:T(8,128)(2,1)} %ow_ref.1, bf16[16,4096]{1,0:T(8,128)(2,1)} %resid_ref.1, f32[1,4096]{1,0:T(1,128)} %bitcast.12, f32[16,128]{1,0:T(8,128)} %select_reduce_fusion.gate_ref, ...), custom_call_target="tpu_custom_call" | custom-call | tf_op jit(solution)/shard_map/layer/pallas_call | solution.py:509
  177.0 0.0 copy-start.1
  177.1 0.0 copy-start
  177.1 4.0 %divide_bitcast_fusion = f32[1,384,1536]{2,1,0:T(8,128)} fusion(f32[384,1536]{1,0:T(8,128)} %get-tuple-element.8, f32[]{:T(128)} %convert_reduce_fusion), kind=kLoop, calls=%fused_computation | loop fusion | flops 589824 | bytes 4718596 | tf_op jit(solution)/shard_map/broadcast_in_dim | solution.py:560
  181.0 0.0 copy-done.1
  181.0 0.7 copy.45
  181.7 0.0 copy-done
  181.7 0.7 copy.46
  (17 shorter events, 0.2 us)
Async XLA Ops:
  177.0 4.0 %copy-start.1 = (bf16[16,4096]{1,0:T(8,128)(2,1)S(1)}, bf16[16,4096]{1,0:T(8,128)(2,1)}, u32[]{:S(2)}) copy-start(bf16[16,4096]{1,0:T(8,128)(2,1)} %get-tuple-element.20) | copy-start | bytes 393220
  177.1 4.6 %copy-start = (f32[16,4096]{1,0:T(8,128)S(1)}, f32[16,4096]{1,0:T(8,128)}, u32[]{:S(2)}) copy-start(f32[16,4096]{1,0:T(8,128)} %get-tuple-element.21) | copy-start | bytes 786436

commit v3 on v2

--- a/solution.py
+++ b/solution.py
@@ -35,13 +35,14 @@
 
 
 def kernel(
-    q_ref, ow_ref, resid_ref, gain_ref, gate_ref, rank_ref, keys_ref, values_ref, wg_ref, wu_ref, wd_ref,
-    mixed_ref, attn_ref, gram_ref,
-    kv, top_s, sum_s, acc_s, h_ref, sel_ref,
-    p1, r10, r11, r12, r13, r14, norm, stream, csh, x0, x1, x2, x3, x4, x5,
-    wgk, wuk, wgs, wus, wdq, xs, psend, precv, hall, p2, r20, r21, r22, r23, r24, fsend, frecv,
+    q_hbm, ow_hbm, resid_hbm, gain_hbm, gate_hbm, rank_hbm, keys_ref, values_ref, wg_ref, wu_ref, wd_ref,
+    mixed_hbm, attn_hbm, gram_hbm,
+    q_ref, resid_ref, gain_ref, gate_ref, rank_ref, mixed_ref, attn_ref, gram_ref, isem, osem,
+    kk, vv, top_s, acc_s, h_ref, sel_ref, ow_ref,
+    p1, r10, r11, r12, r13, norm, stream, csh, x0, x1, x2, x3, x4, x5,
+    wgk, wuk, wgs, wus, wdq, xs, psend, precv, hall, p2, r20, r21, r22, r23, frecv,
     kvl, kvs, kvr,
-    s1s, s1r, wss, wsr, lsem, ccs, ccr, ags, agr, pss, psr, hss, hsr, has, har, s2s, s2r, fss, fsr,
+    s1s, s1r, t1s, t1r, wss, wsr, lsem, ccs, ccr, ags, agr, pss, psr, hss, hsr, has, har, s2s, s2r, fss, fsr,
 ):
     c = lax.axis_index("ctx")
     e = lax.axis_index("exp")
@@ -61,13 +62,26 @@
     far = dev(x, y, zl, 1 - zh, k)
     farsib = dev(x, y, zl, 1 - zh, 1 - k)
     rs_peer = (peer_x[0], peer_x[1], peer_y[0], peer_y[1], peer_z1)
+    diagonal = (
+        dev(3 - x, y, 1 - zl, zh, k), dev(flip1(x), y, 1 - zl, zh, k),
+        dev(x, 3 - y, 1 - zl, zh, k), dev(x, flip1(y), 1 - zl, zh, k),
+    )
+    z1sib, z3sib = dev(x, y, 1 - zl, zh, 1 - k), dev(x, y, 1 - zl, 1 - zh, 1 - k)
     ag_peer = (peer_x[0], peer_x[1], peer_y[0], peer_y[1], peer_z3, peer_z1)
     xb1, yb1 = x // 2, y // 2
     own5 = (xb1, (xb1 + x % 2) % 2, yb1, (yb1 + y % 2) % 2, zl)
     own6 = own5[:4] + (zh, (zh + zl) % 2)
 
+    hbm_vmem = (
+        (q_hbm, q_ref), (rank_hbm, rank_ref), (ow_hbm, ow_ref), (resid_hbm, resid_ref), (gain_hbm, gain_ref),
+        (gate_hbm, gate_ref),
+    )
+    input_copies = [pltpu.make_async_copy(a, b, isem.at[i]) for i, (a, b) in enumerate(hbm_vmem)]
+    attn_copy = pltpu.make_async_copy(attn_ref, attn_hbm, osem.at[0])
+    gram_copy = pltpu.make_async_copy(gram_ref, gram_hbm, osem.at[1])
+    mixed_copy = pltpu.make_async_copy(mixed_ref, mixed_hbm, osem.at[2])
     barrier = pltpu.get_barrier_semaphore()
-    partners = list(ag_peer) + [sib, far, farsib]
+    partners = list(ag_peer) + [sib, far, farsib, z1sib, z3sib] + list(diagonal)
     for p in partners:
         pl.semaphore_signal(barrier, inc=1, device_id=p, device_id_type=MESH)
     pl.semaphore_wait(barrier, len(partners))
@@ -80,15 +94,23 @@
     head_cols = pl.ds(pl.multiple_of(x * HEAD_SIZE, HEAD_SIZE), HEAD_SIZE)
     kv_src = (keys_ref.at[:, head_cols], values_ref.at[:, head_cols])
 
+    def kv_dst(cc, j):
+        return vv.at[cc, :, 0:HEAD_SIZE] if j else kk.at[cc]
+
     def kv_copy(i, to, cc, j):
-        return remote(kv_src[j], kv.at[cc, j], kvs.at[i, j], kvr.at[cc, j], to)
+        return remote(kv_src[j], kv_dst(cc, j), kvs.at[i, j], kvr.at[cc, j], to)
+
+    def kv_local(j):
+        return pltpu.make_async_copy(kv_src[j], kv_dst(c, j), kvl.at[j])
+
+    def kv_forward(j):
+        return remote(kv_dst(k, j), kv_dst(k, j), kvs.at[2, j], kvr.at[k, j], sib)
 
     for j in range(2):
 
         @pl.when(zh == 0)
         def _():
-            kv_copy(1, far, c, j).start()
-            kv_copy(2, farsib, c, j).start()
+            kv_copy(1, peer_z3, c, j).start()
 
     for j in range(2):
 
@@ -96,53 +118,102 @@
         def _():
             kv_copy(0, sib, c, j).start()
 
-        pltpu.make_async_copy(kv_src[j], kv.at[c, j], kvl.at[j]).start()
+        kv_local(j).start()
+
+    for cp in input_copies:
+        cp.start()
+
+    other = pl.ds(pl.multiple_of((1 - k) * HALF, HALF), HALF)
+    mine = pl.ds(pl.multiple_of(k * HALF, HALF), HALF)
+    own_rows = pl.ds(pl.multiple_of(c * FFS, FFS), FFS)
+
+    def quarter(cc):
+        return pl.ds(pl.multiple_of(cc * QUART, QUART), QUART)
+
+    near_copies = [
+        remote(wg_ref.at[other], wgs, wss.at[0], wsr.at[0], sib),
+        remote(wu_ref.at[other], wus, wss.at[1], wsr.at[1], sib),
+        remote(wd_ref.at[:, quarter(zh * 2 + 1 - k)], wdq.at[own_rows], wss.at[2], wsr.at[2], sib),
+        pltpu.make_async_copy(wg_ref.at[mine], wgk, lsem.at[0]),
+        pltpu.make_async_copy(wu_ref.at[mine], wuk, lsem.at[1]),
+        pltpu.make_async_copy(wd_ref.at[:, quarter(c)], wdq.at[own_rows], lsem.at[2]),
+    ]
+    far_copies = [
+        remote(wd_ref.at[:, quarter((1 - zh) * 2 + k)], wdq.at[own_rows], wss.at[3], wsr.at[3], far),
+        remote(wd_ref.at[:, quarter((1 - zh) * 2 + 1 - k)], wdq.at[own_rows], wss.at[4], wsr.at[4], farsib),
+    ]
+
+    @pl.when(zh == 1)
+    def _():
+        for cp in far_copies:
+            cp.start()
 
     slot = lax.broadcasted_iota(jnp.int32, (128, 256), 0)
     token = lax.broadcasted_iota(jnp.int32, (128, 256), 1)
     place = jnp.where(slot // 8 == token // 16, slot % 8, -2)
 
+    for cp in input_copies[:2]:
+        cp.wait()
+
     def pick_slots(g):
         sel_ref[g] = jnp.where(place == rank_ref[g], 1.0, 0.0).astype(BF)
 
     pl.loop(0, 8)(pick_slots)
-    top_s[...] = jnp.full((4, 256, 1), -1e30, F32)
-    sum_s[...] = jnp.zeros((4, 256, 1), F32)
-    acc_s[...] = jnp.zeros((4, 256, HEAD_SIZE), F32)
+    for cc in range(4):
+        vv[cc, :, HEAD_SIZE:] = jnp.ones((512, HEAD_SIZE), BF)
+    scale = math.log2(math.e) / math.sqrt(HEAD_SIZE)
+    trans = (((1,), (1,)), ((), ()))
+
+    def queries(t):
+        rows = slice(t * 128, t * 128 + 128)
+        return jnp.concatenate([q_ref[rows, :HEAD_SIZE], q_ref[rows, HEAD_SIZE:]], axis=0)
+
     for j in range(2):
-        pltpu.make_async_copy(kv_src[j], kv.at[c, j], kvl.at[j]).wait()
-    q_place = lax.rem(lax.broadcasted_iota(jnp.int32, (256, 512), 0), 128)
-    k_place = lax.broadcasted_iota(jnp.int32, (256, 512), 1)
-    scale = 1.0 / math.sqrt(HEAD_SIZE)
+        kv_local(j).wait()
+    for cp in near_copies:
+        cp.start()
+    for t in range(4):
+        n = t * 128 + 128
+        scores = lax.dot_general(queries(t), kk[c, :n], trans, preferred_element_type=F32)
+        q_place = lax.rem(lax.broadcasted_iota(jnp.int32, (256, n), 0), 128) + t * 128
+        scores = jnp.where(q_place >= lax.broadcasted_iota(jnp.int32, (256, n), 1), scores, -1e30)
+        new = jnp.max(scores, axis=1, keepdims=True)
+        w = jnp.exp2((scores - new) * scale).astype(BF)
+        top_s[t] = new
+        acc_s[t] = jnp.dot(w, vv[c, :n], preferred_element_type=F32)
+
+    @pl.when(zh == 1)
+    def _():
+        for j in range(2):
+            kv_copy(1, peer_z3, k, j).wait_recv()
+            kv_forward(j).start()
 
     def key_block(i):
         cc = c - i
 
-        @pl.when(i > 0)
+        @pl.when(jnp.logical_or(zh == 0, cc != k))
         def _():
             for j in range(2):
                 kv_copy(0, sib, cc, j).wait_recv()
 
-        def tile(t):
-            rows = pl.ds(pl.multiple_of(t * 128, 128), 128)
-            q = jnp.concatenate([q_ref[rows, :HEAD_SIZE], q_ref[rows, HEAD_SIZE:]], axis=0)
-            scores = lax.dot_general(q, kv[cc, 0], (((1,), (1,)), ((), ())), preferred_element_type=F32) * scale
-            allowed = q_place + (t * 128 + i * 512) >= k_place
-            scores = jnp.where(allowed, scores, -1e30)
+        for t in range(4):
+            scores = lax.dot_general(queries(t), kk[cc], trans, preferred_element_type=F32)
             old = top_s[t]
             new = jnp.maximum(old, jnp.max(scores, axis=1, keepdims=True))
-            w = jnp.where(allowed, jnp.exp(scores - new), 0.0).astype(BF)
-            fade = jnp.exp(old - new)
+            w = jnp.exp2((scores - new) * scale).astype(BF)
+            fade = jnp.exp2((old - new) * scale)
             top_s[t] = new
-            sum_s[t] = sum_s[t] * fade + jnp.sum(w.astype(F32), axis=1, keepdims=True)
-            acc_s[t] = acc_s[t] * fade + jnp.dot(w, kv[cc, 1], preferred_element_type=F32)
-
-        pl.loop(0, 4)(tile)
-
-    pl.loop(0, c + 1)(key_block)
+            acc_s[t] = acc_s[t] * fade + jnp.dot(w, vv[cc], preferred_element_type=F32)
+
+    pl.loop(1, c + 1)(key_block)
+
+    @pl.when(zh == 0)
+    def _():
+        for cp in far_copies:
+            cp.start()
 
     def head_tile(t):
-        out = (acc_s[t] / sum_s[t]).astype(BF)
+        out = (acc_s[t, :, :HEAD_SIZE] / acc_s[t, :, HEAD_SIZE:]).astype(BF)
         b1 = t // 2
         b0 = (b1 + t % 2) % 2
         for hd in range(2):
@@ -187,8 +258,8 @@
         else:
             one(0)
 
-    recv1 = (r10, r11, r12, r13, r14)
-    recv2 = (r20, r21, r22, r23, r24)
+    recv1 = (r10, r11, r12)
+    recv2 = (r20, r21, r22, r23)
 
     def project(f, bit):
         idx = rs_index(f, 0, bit)
@@ -198,6 +269,8 @@
             out = jnp.dot(rows, ow_ref[:, cols : cols + 512], preferred_element_type=F32)
             p1[(f,) + idx + (FULL, slice(t * 512, t * 512 + 512))] = out.astype(BF).reshape(2, 2, 2, 2, 16, 512)
 
+    for cp in input_copies[2:]:
+        cp.wait()
     first = []
     for f in range(4):
         project(f, 1 - own5[RS_ORDER[f][0]])
@@ -205,44 +278,25 @@
         cp.start()
         first.append(cp)
 
-    other = pl.ds(pl.multiple_of((1 - k) * HALF, HALF), HALF)
-    mine = pl.ds(pl.multiple_of(k * HALF, HALF), HALF)
-    own_rows = pl.ds(pl.multiple_of(c * FFS, FFS), FFS)
-
-    def quarter(cc):
-        return pl.ds(pl.multiple_of(cc * QUART, QUART), QUART)
-
-    weight_copies = [
-        remote(wg_ref.at[other], wgs, wss.at[0], wsr.at[0], sib),
-        remote(wu_ref.at[other], wus, wss.at[1], wsr.at[1], sib),
-        remote(wd_ref.at[:, quarter(zh * 2 + 1 - k)], wdq.at[own_rows], wss.at[2], wsr.at[2], sib),
-        remote(wd_ref.at[:, quarter((1 - zh) * 2 + k)], wdq.at[own_rows], wss.at[3], wsr.at[3], far),
-        remote(wd_ref.at[:, quarter((1 - zh) * 2 + 1 - k)], wdq.at[own_rows], wss.at[4], wsr.at[4], farsib),
-    ]
-    local_copies = [
-        pltpu.make_async_copy(wg_ref.at[mine], wgk, lsem.at[0]),
-        pltpu.make_async_copy(wu_ref.at[mine], wuk, lsem.at[1]),
-        pltpu.make_async_copy(wd_ref.at[:, quarter(c)], wdq.at[own_rows], lsem.at[2]),
-    ]
-    for cp in weight_copies + local_copies:
-        cp.start()
-
     for f in range(4):
         project(f, own5[RS_ORDER[f][0]])
     for j in range(2):
 
         @pl.when(zh == 0)
         def _():
-            kv_copy(1, far, c, j).wait_send()
-            kv_copy(2, farsib, c, j).wait_send()
+            kv_copy(1, peer_z3, c, j).wait_send()
+
+        @pl.when(zh == 1)
+        def _():
+            kv_forward(j).wait_send()
 
         @pl.when(k == 0)
         def _():
             kv_copy(0, sib, c, j).wait_send()
 
-    def finish_rs(buf, recv, ss, rs, wait_first):
+    def run_rs(buf, recv, ss, rs, wait_first, steps, tail):
         last = [None] * 4
-        for s in range(4):
+        for s in range(steps):
             for f in range(4):
                 if s == 0:
                     wait_first(f)
@@ -250,16 +304,30 @@
                     last[f].wait()
                 d = RS_ORDER[f][s + 1]
                 rs_add(buf, recv, f, s, 1 - own5[d])
-                last[f] = rs_copy(buf, recv, ss, rs, f, s + 1)
-                last[f].start()
+                if s + 1 < steps:
+                    last[f] = rs_copy(buf, recv, ss, rs, f, s + 1)
+                    last[f].start()
                 rs_add(buf, recv, f, s, own5[d])
-        out = []
-        for f in range(4):
-            last[f].wait()
-            out.append(buf[(f,) + own5].astype(F32) + recv[4][f].astype(F32))
-        return out
-
-    parts = finish_rs(p1, recv1, s1s, s1r, lambda f: first[f].wait())
+                if s + 1 == steps:
+                    tail(f)
+
+    tails = []
+
+    def direct(f):
+        d = RS_ORDER[f][3]
+        for i, (to, flips) in enumerate(((rs_peer[d], (d,)), (peer_z1, (4,)), (diagonal[d], (d, 4)))):
+            idx = tuple(1 - own5[j] if j in flips else own5[j] for j in range(5))
+            cp = remote(p1.at[(f,) + idx], r13.at[f, i], t1s.at[f, i], t1r.at[f, i], to)
+            cp.start()
+            tails.append(cp)
+
+    run_rs(p1, recv1, s1s, s1r, lambda f: first[f].wait(), 3, direct)
+    parts = []
+    for f in range(4):
+        for i in range(3):
+            tails[f * 3 + i].wait()
+        got = [r13[f, i].astype(F32) for i in range(3)]
+        parts.append((p1[(f,) + own5].astype(F32) + got[0]) + (got[1] + got[2]))
 
     squares = jnp.zeros((16, 1), F32)
     for f in range(4):
@@ -269,6 +337,7 @@
         stream[:, cols] = st
         sf = st.astype(F32)
         squares = squares + jnp.sum(sf * sf, axis=1, keepdims=True)
+    attn_copy.start()
     inv = lax.rsqrt(squares / D + 1e-06)
     for f in range(4):
         cols = slice(f * 1024, f * 1024 + 1024)
@@ -321,7 +390,7 @@
             for j in range(-1, s):
                 ag_copy(f, s, j).wait_send()
 
-    for cp in weight_copies + local_copies:
+    for cp in near_copies + far_copies:
         cp.wait()
 
     def chunk_bits(i):
@@ -370,17 +439,12 @@
         hidden_copy(m, c, 1, sib).start()
 
     def units(i):
-        @pl.when(i < 4)
-        def _():
-            m = chunk(i)
-            select(m)
-            other_units(m)
-
-        @pl.when(i > 0)
-        def _():
-            own_units(chunk(i - 1))
-
-    pl.loop(0, 5)(units)
+        m = chunk(i)
+        select(m)
+        other_units(m)
+        own_units(m)
+
+    pl.loop(0, 4)(units)
     far_c = (1 - zh) * 2 + k
 
     def half_copy(f, b1, b0):
@@ -450,61 +514,82 @@
             else:
                 half_copy(f, b // 2, b % 2).wait()
 
+    count = jnp.sum(jnp.where(rank_ref[:, 0, :] >= 0, 1.0, 0.0))
+
     def gram(j):
         cols = pl.ds(pl.multiple_of(j * 256, 256), 256)
-        gram_ref[:, cols] = lax.dot_general(
+        out = lax.dot_general(
             hall[:, hidden_cols(c)], hall[:, cols], (((0,), (0,)), ((), ())), preferred_element_type=F32
         )
+        gram_ref[:, cols] = out / count
 
     pl.loop(0, 6)(gram)
-
-    parts = finish_rs(p2, recv2, s2s, s2r, wait_half)
-    for f in range(4):
-        cols = slice(f * 256, f * 256 + 256)
-        fsend[:, :, cols] = parts[f].astype(BF).reshape(4, 16, 256)
+    gram_copy.start()
+
+    def nothing(f):
+        return None
+
+    run_rs(p2, recv2, s2s, s2r, wait_half, 4, nothing)
     final = []
-    for i, (cc, to) in enumerate(
-        ((zh * 2 + 1 - k, sib), ((1 - zh) * 2 + k, far), ((1 - zh) * 2 + 1 - k, farsib))
+    for i, (to, (flip_l, flip_h, flip_k)) in enumerate(
+        (
+            (sib, (0, 0, 1)), (peer_z1, (1, 0, 0)), (far, (0, 1, 0)), (peer_z3, (1, 1, 0)),
+            (z1sib, (1, 0, 1)), (farsib, (0, 1, 1)), (z3sib, (1, 1, 1)),
+        )
     ):
-        cp = remote(fsend.at[cc], frecv.at[c], fss.at[i], fsr.at[i], to)
+        to_l = 1 - zl if flip_l else zl
+        to_c = (1 - zh if flip_h else zh) * 2 + (1 - k if flip_k else k)
+        rows = pl.ds(pl.multiple_of(to_c * 16, 16), 16)
+        cp = remote(p2.at[(FULL,) + own5[:4] + (to_l, rows)], frecv.at[zl, c], fss.at[i], fsr.at[i], to)
         cp.start()
         final.append(cp)
-    frecv[c] = fsend[c]
+    rows = pl.ds(pl.multiple_of(c * 16, 16), 16)
+    frecv[zl, c] = p2[(FULL,) + own5 + (rows,)]
     for cp in final:
         cp.wait()
     for cc in range(4):
-        cols = slice(cc * QUART, cc * QUART + QUART)
-        mixed_ref[:, cols] = (stream[:, cols].astype(F32) + frecv[cc].astype(F32)).astype(BF)
+        for f in range(4):
+            cols = slice(cc * QUART + f * 256, cc * QUART + f * 256 + 256)
+            routed = frecv[0, cc, f].astype(F32) + frecv[1, cc, f].astype(F32)
+            mixed_ref[:, cols] = (stream[:, cols].astype(F32) + routed).astype(BF)
+    mixed_copy.start()
+    attn_copy.wait()
+    gram_copy.wait()
+    mixed_copy.wait()
 
 
 def fused(q, ow, resid, gain, gate, rank, keys, values, wg, wu, wd):
     dma = pltpu.SemaphoreType.DMA
-    vm = pl.BlockSpec(memory_space=pltpu.VMEM)
     hbm = pl.BlockSpec(memory_space=pl.ANY)
     two = (2,) * 6
 
-    def rs_scratch(rows, cols):
+    def rs_scratch(rows, cols, steps):
         out = [pltpu.VMEM((4,) + (2,) * 5 + (rows, cols), BF)]
-        for s in range(5):
+        for s in range(steps):
             out.append(pltpu.VMEM((4,) + (2,) * (4 - s) + (rows, cols), BF))
         return out
 
     scratch = (
-        [pltpu.VMEM((4, 2, 512, HEAD_SIZE), BF), pltpu.VMEM((4, 256, 1), F32), pltpu.VMEM((4, 256, 1), F32)]
-        + [pltpu.VMEM((4, 256, HEAD_SIZE), F32), pltpu.VMEM((2,) * 5 + (16, 256), BF), pltpu.VMEM((8, 128, 256), BF)]
-        + rs_scratch(16, 1024)
+        [pltpu.VMEM((512, 256), BF), pltpu.VMEM((16, D), BF), pltpu.VMEM((1, D), F32), pltpu.VMEM((16, 128), F32)]
+        + [pltpu.VMEM((8, 1, 256), jnp.int32), pltpu.VMEM((16, D), BF), pltpu.VMEM((16, D), F32)]
+        + [pltpu.VMEM((FFS, FF), F32), dma((6,)), dma((3,))]
+        + [pltpu.VMEM((4, 512, HEAD_SIZE), BF), pltpu.VMEM((4, 512, 2 * HEAD_SIZE), BF), pltpu.VMEM((4, 256, 1), F32)]
+        + [pltpu.VMEM((4, 256, 2 * HEAD_SIZE), F32), pltpu.VMEM((2,) * 5 + (16, 256), BF), pltpu.VMEM((8, 128, 256), BF)]
+        + [pltpu.VMEM((256, D), BF)]
+        + rs_scratch(16, 1024, 3)
+        + [pltpu.VMEM((4, 3, 16, 1024), BF)]
         + [pltpu.VMEM((2, 16, WIDE), BF), pltpu.VMEM((16, D), BF), pltpu.VMEM((16, WIDE), BF)]
         + [pltpu.VMEM(two + (32, w), BF) for w in WIDTHS]
         + [pltpu.VMEM((HALF, FFS), BF)] * 4
         + [pltpu.VMEM((FF, QUART), BF), pltpu.VMEM((1024, HALF), BF)]
         + [pltpu.VMEM((4, 256, 2 * FFS), BF)] * 2
         + [pltpu.VMEM((1024, FF), BF)]
-        + rs_scratch(64, 256)
-        + [pltpu.VMEM((4, 16, QUART), BF)] * 2
+        + rs_scratch(64, 256, 4)
+        + [pltpu.VMEM((2, 4, 4, 16, 256), BF)]
         + [dma((2,)), dma((3, 2)), dma((4, 2))]
-        + [dma((4, 5)), dma((4, 5)), dma((5,)), dma((5,)), dma((3,)), dma((1,)), dma((1,))]
+        + [dma((4, 3)), dma((4, 3)), dma((4, 3)), dma((4, 3)), dma((5,)), dma((5,)), dma((3,)), dma((1,)), dma((1,))]
         + [dma((6, 6, 6)), dma((6, 6, 6)), dma((4,)), dma((4,)), dma((3, 4)), dma((3, 4))]
-        + [dma((4, 4)), dma((4, 4)), dma((4, 5)), dma((4, 5)), dma((3,)), dma((3,))]
+        + [dma((4, 4)), dma((4, 4)), dma((4, 4)), dma((4, 4)), dma((7,)), dma((7,))]
     )
     return pl.pallas_call(
         kernel,
@@ -513,8 +598,8 @@
             jax.ShapeDtypeStruct((16, D), F32),
             jax.ShapeDtypeStruct((FFS, FF), F32),
         ),
-        in_specs=[vm] * 6 + [hbm] * 5,
-        out_specs=(vm, vm, vm),
+        in_specs=[hbm] * 11,
+        out_specs=(hbm, hbm, hbm),
         scratch_shapes=scratch,
         compiler_params=pltpu.CompilerParams(
             collective_id=0, has_side_effects=True, vmem_limit_bytes=62 * 2**20
@@ -549,7 +634,6 @@
     expert = jnp.where(expert < 3 * EXPERTS, expert % EXPERTS, -1)
     gate = jnp.sum(jnp.where(own_idx[:, :, None] == expert[None, None, :], gates[:, :, None], 0.0), axis=1)
     member = jnp.any(route_idx == exp_pos, axis=1)
-    count = jnp.sum(member.astype(F32))
     member = gathered_order(member.astype(BF)).reshape(128, 16)
     before = (jnp.arange(16)[:, None] < jnp.arange(16)[None, :]).astype(BF)
     rank = jnp.dot(member, before, preferred_element_type=F32)
@@ -557,7 +641,7 @@
     mixed, attn_out, gram = fused(
         query, out_weight, resid, post_gain.reshape(1, D), gate, rank, keys, values, w_gate[0], w_up[0], w_down[0]
     )
-    return (mixed, attn_out, (gram / count)[None])
+    return (mixed, attn_out, gram[None])
 
 
 def solution(mesh):

time: 183 us -> 201 us (1.098)
  Pallas kernels: 171 us -> 189 us
  local copies, waits for them, and re-layouts: 4.49 us -> 9.59 us
  other arithmetic: 6.29 us -> 1.65 us
    pallas_call x1, Pallas kernels: 171 us -> 189 us  [fused(): pl.pallas_call(kernel, out_shape=(jax.ShapeDtypeStruct((16, D), BF), jax....]
    unnamed x10 -> x7, local copies, waits for them, and re-layouts: 2.15 us -> 7.24 us
    broadcast_in_dim x1 -> x0, other arithmetic: 3.97 us -> none  [local(): return (mixed, attn_out, (gram / count)[None])]
where the time goes in v3:
time: 201 us
  Pallas kernels  189 us (94%)
  local copies, waits for them, and re-layouts  9.59 us (5%)
    pallas_call x1, Pallas kernels, fused(): pl.pallas_call(kernel, out_shape=(jax.ShapeDtypeStruct((16, D), BF), jax....  189 us
    unnamed x7, local copies, waits for them, and re-layouts  7.24 us

profile of v3, /device:TPU:1, one launch (start us, length us, event | category | flops | bytes accessed | tf_op | source)
XLA Modules:
  0.0 201.0 jit_solution(16924346075054768997)
XLA Ops:
  0.6 0.9 compare_reduce_fusion
  1.5 0.8 constant_dynamic-slice_fusion
  2.3 0.1 copy.31
  2.4 0.8 copy.32
  3.1 0.7 select_reduce_fusion.gate_hbm
  3.8 0.1 reshape.37
  4.0 0.1 slice.53
  4.1 0.1 slice.51
  4.2 0.1 slice.49
  4.3 0.1 slice.47
  4.5 0.1 reshape_reshape.3
  4.6 0.1 copy.37
  4.7 0.2 fusion
  4.9 0.1 copy.38
  5.0 0.7 reshape.38.rank_hbm
  5.7 188.8 %layer.1 = (bf16[16,4096]{1,0:T(8,128)(2,1)}, f32[16,4096]{1,0:T(8,128)}, f32[384,1536]{1,0:T(8,128)}) custom-call(bf16[512,256]{1,0:T(8,128)(2,1)} %q_hbm.1, bf16[256,4096]{1,0:T(8,128)(2,1)} %ow_hbm.1, bf16[16,4096]{1,0:T(8,128)(2,1)} %resid_hbm.1, f32[1,4096]{1,0:T(1,128)} %bitcast.12, f32[16,128]{1,0:T(8,128)} %select_reduce_fusion.gate_hbm, ...), custom_call_target="tpu_custom_call" | custom-call | tf_op jit(solution)/shard_map/layer/pallas_call | solution.py:594
  194.5 1.6 copy.46
  196.1 1.7 copy.47
  197.8 3.2 %copy.48 = f32[1,384,1536]{2,1,0:T(8,128)} copy(f32[1,384,1536]{2,1,0:T(8,128)} %bitcast.10) | data formatting | bytes 4718592
  (17 shorter events, 0.2 us)

commit v4 on v3

--- a/solution.py
+++ b/solution.py
@@ -36,8 +36,8 @@
 
 def kernel(
     q_hbm, ow_hbm, resid_hbm, gain_hbm, gate_hbm, rank_hbm, keys_ref, values_ref, wg_ref, wu_ref, wd_ref,
-    mixed_hbm, attn_hbm, gram_hbm,
-    q_ref, resid_ref, gain_ref, gate_ref, rank_ref, mixed_ref, attn_ref, gram_ref, isem, osem,
+    mixed_ref, attn_ref, gram_hbm,
+    q_ref, resid_ref, gain_ref, gate_ref, rank_ref, gram_ref, isem, osem,
     kk, vv, top_s, acc_s, h_ref, sel_ref, ow_ref,
     p1, r10, r11, r12, r13, norm, stream, csh, x0, x1, x2, x3, x4, x5,
     wgk, wuk, wgs, wus, wdq, xs, psend, precv, hall, p2, r20, r21, r22, r23, frecv,
@@ -77,9 +77,7 @@
         (gate_hbm, gate_ref),
     )
     input_copies = [pltpu.make_async_copy(a, b, isem.at[i]) for i, (a, b) in enumerate(hbm_vmem)]
-    attn_copy = pltpu.make_async_copy(attn_ref, attn_hbm, osem.at[0])
-    gram_copy = pltpu.make_async_copy(gram_ref, gram_hbm, osem.at[1])
-    mixed_copy = pltpu.make_async_copy(mixed_ref, mixed_hbm, osem.at[2])
+    gram_copy = pltpu.make_async_copy(gram_ref, gram_hbm, osem.at[0])
     barrier = pltpu.get_barrier_semaphore()
     partners = list(ag_peer) + [sib, far, farsib, z1sib, z3sib] + list(diagonal)
     for p in partners:
@@ -170,8 +168,6 @@
 
     for j in range(2):
         kv_local(j).wait()
-    for cp in near_copies:
-        cp.start()
     for t in range(4):
         n = t * 128 + 128
         scores = lax.dot_general(queries(t), kk[c, :n], trans, preferred_element_type=F32)
@@ -187,6 +183,9 @@
         for j in range(2):
             kv_copy(1, peer_z3, k, j).wait_recv()
             kv_forward(j).start()
+
+    for cp in near_copies:
+        cp.start()
 
     def key_block(i):
         cc = c - i
@@ -337,7 +336,6 @@
         stream[:, cols] = st
         sf = st.astype(F32)
         squares = squares + jnp.sum(sf * sf, axis=1, keepdims=True)
-    attn_copy.start()
     inv = lax.rsqrt(squares / D + 1e-06)
     for f in range(4):
         cols = slice(f * 1024, f * 1024 + 1024)
@@ -439,12 +437,17 @@
         hidden_copy(m, c, 1, sib).start()
 
     def units(i):
-        m = chunk(i)
-        select(m)
-        other_units(m)
-        own_units(m)
-
-    pl.loop(0, 4)(units)
+        @pl.when(i < 4)
+        def _():
+            m = chunk(i)
+            select(m)
+            other_units(m)
+
+        @pl.when(i > 0)
+        def _():
+            own_units(chunk(i - 1))
+
+    pl.loop(0, 5)(units)
     far_c = (1 - zh) * 2 + k
 
     def half_copy(f, b1, b0):
@@ -552,14 +555,12 @@
             cols = slice(cc * QUART + f * 256, cc * QUART + f * 256 + 256)
             routed = frecv[0, cc, f].astype(F32) + frecv[1, cc, f].astype(F32)
             mixed_ref[:, cols] = (stream[:, cols].astype(F32) + routed).astype(BF)
-    mixed_copy.start()
-    attn_copy.wait()
     gram_copy.wait()
-    mixed_copy.wait()
 
 
 def fused(q, ow, resid, gain, gate, rank, keys, values, wg, wu, wd):
     dma = pltpu.SemaphoreType.DMA
+    vm = pl.BlockSpec(memory_space=pltpu.VMEM)
     hbm = pl.BlockSpec(memory_space=pl.ANY)
     two = (2,) * 6
 
@@ -571,8 +572,7 @@
 
     scratch = (
         [pltpu.VMEM((512, 256), BF), pltpu.VMEM((16, D), BF), pltpu.VMEM((1, D), F32), pltpu.VMEM((16, 128), F32)]
-        + [pltpu.VMEM((8, 1, 256), jnp.int32), pltpu.VMEM((16, D), BF), pltpu.VMEM((16, D), F32)]
-        + [pltpu.VMEM((FFS, FF), F32), dma((6,)), dma((3,))]
+        + [pltpu.VMEM((8, 1, 256), jnp.int32), pltpu.VMEM((FFS, FF), F32), dma((6,)), dma((1,))]
         + [pltpu.VMEM((4, 512, HEAD_SIZE), BF), pltpu.VMEM((4, 512, 2 * HEAD_SIZE), BF), pltpu.VMEM((4, 256, 1), F32)]
         + [pltpu.VMEM((4, 256, 2 * HEAD_SIZE), F32), pltpu.VMEM((2,) * 5 + (16, 256), BF), pltpu.VMEM((8, 128, 256), BF)]
         + [pltpu.VMEM((256, D), BF)]
@@ -599,7 +599,7 @@
             jax.ShapeDtypeStruct((FFS, FF), F32),
         ),
         in_specs=[hbm] * 11,
-        out_specs=(hbm, hbm, hbm),
+        out_specs=(vm, vm, hbm),
         scratch_shapes=scratch,
         compiler_params=pltpu.CompilerParams(
             collective_id=0, has_side_effects=True, vmem_limit_bytes=62 * 2**20

time: 201 us -> 197 us (0.980)
  Pallas kernels: 189 us -> 185 us
    pallas_call x1, Pallas kernels: 189 us -> 185 us  [fused(): pl.pallas_call(kernel, out_shape=(jax.ShapeDtypeStruct((16, D), BF), jax....]
where the time goes in v4:
time: 197 us
  Pallas kernels  185 us (94%)
  local copies, waits for them, and re-layouts  9.59 us (5%)
    pallas_call x1, Pallas kernels, fused(): pl.pallas_call(kernel, out_shape=(jax.ShapeDtypeStruct((16, D), BF), jax....  185 us
    unnamed x7, local copies, waits for them, and re-layouts  7.24 us

profile of v4, /device:TPU:1, one launch (start us, length us, event | category | flops | bytes accessed | tf_op | source)
XLA Modules:
  0.0 197.1 jit_solution(17676080463650236726)
XLA Ops:
  0.6 0.9 compare_reduce_fusion
  1.5 0.8 constant_dynamic-slice_fusion
  2.3 0.1 copy.31
  2.4 0.8 copy.32
  3.1 0.7 select_reduce_fusion.gate_hbm
  3.8 0.1 reshape.37
  4.0 0.1 slice.53
  4.1 0.1 slice.51
  4.2 0.1 slice.49
  4.3 0.1 slice.47
  4.5 0.1 reshape_reshape.3
  4.6 0.1 copy.37
  4.7 0.2 fusion
  4.9 0.1 copy.38
  5.0 0.7 reshape.38.rank_hbm
  5.7 185.0 %layer.1 = (bf16[16,4096]{1,0:T(8,128)(2,1)}, f32[16,4096]{1,0:T(8,128)}, f32[384,1536]{1,0:T(8,128)}) custom-call(bf16[512,256]{1,0:T(8,128)(2,1)} %q_hbm.1, bf16[256,4096]{1,0:T(8,128)(2,1)} %ow_hbm.1, bf16[16,4096]{1,0:T(8,128)(2,1)} %resid_hbm.1, f32[1,4096]{1,0:T(1,128)} %bitcast.12, f32[16,128]{1,0:T(8,128)} %select_reduce_fusion.gate_hbm, ...), custom_call_target="tpu_custom_call" | custom-call | tf_op jit(solution)/shard_map/layer/pallas_call | solution.py:594
  190.7 1.6 copy.46
  192.3 1.7 copy.47
  193.9 3.2 %copy.48 = f32[1,384,1536]{2,1,0:T(8,128)} copy(f32[1,384,1536]{2,1,0:T(8,128)} %bitcast.10) | data formatting | bytes 4718592
  (17 shorter events, 0.2 us)

commit v5 on v4

--- a/solution.py
+++ b/solution.py
@@ -36,8 +36,8 @@
 
 def kernel(
     q_hbm, ow_hbm, resid_hbm, gain_hbm, gate_hbm, rank_hbm, keys_ref, values_ref, wg_ref, wu_ref, wd_ref,
-    mixed_ref, attn_ref, gram_hbm,
-    q_ref, resid_ref, gain_ref, gate_ref, rank_ref, gram_ref, isem, osem,
+    mixed_ref, attn_ref, gram_ref,
+    q_ref, resid_ref, gain_ref, gate_ref, rank_ref, isem,
     kk, vv, top_s, acc_s, h_ref, sel_ref, ow_ref,
     p1, r10, r11, r12, r13, norm, stream, csh, x0, x1, x2, x3, x4, x5,
     wgk, wuk, wgs, wus, wdq, xs, psend, precv, hall, p2, r20, r21, r22, r23, frecv,
@@ -77,7 +77,6 @@
         (gate_hbm, gate_ref),
     )
     input_copies = [pltpu.make_async_copy(a, b, isem.at[i]) for i, (a, b) in enumerate(hbm_vmem)]
-    gram_copy = pltpu.make_async_copy(gram_ref, gram_hbm, osem.at[0])
     barrier = pltpu.get_barrier_semaphore()
     partners = list(ag_peer) + [sib, far, farsib, z1sib, z3sib] + list(diagonal)
     for p in partners:
@@ -108,7 +107,8 @@
 
         @pl.when(zh == 0)
         def _():
-            kv_copy(1, peer_z3, c, j).start()
+            kv_copy(1, far, c, j).start()
+            kv_copy(2, farsib, c, j).start()
 
     for j in range(2):
 
@@ -178,22 +178,14 @@
         top_s[t] = new
         acc_s[t] = jnp.dot(w, vv[c, :n], preferred_element_type=F32)
 
-    @pl.when(zh == 1)
-    def _():
-        for j in range(2):
-            kv_copy(1, peer_z3, k, j).wait_recv()
-            kv_forward(j).start()
-
     for cp in near_copies:
         cp.start()
 
     def key_block(i):
         cc = c - i
 
-        @pl.when(jnp.logical_or(zh == 0, cc != k))
-        def _():
-            for j in range(2):
-                kv_copy(0, sib, cc, j).wait_recv()
+        for j in range(2):
+            kv_copy(0, sib, cc, j).wait_recv()
 
         for t in range(4):
             scores = lax.dot_general(queries(t), kk[cc], trans, preferred_element_type=F32)
@@ -283,11 +275,8 @@
 
         @pl.when(zh == 0)
         def _():
-            kv_copy(1, peer_z3, c, j).wait_send()
-
-        @pl.when(zh == 1)
-        def _():
-            kv_forward(j).wait_send()
+            kv_copy(1, far, c, j).wait_send()
+            kv_copy(2, farsib, c, j).wait_send()
 
         @pl.when(k == 0)
         def _():
@@ -517,17 +506,14 @@
             else:
                 half_copy(f, b // 2, b % 2).wait()
 
-    count = jnp.sum(jnp.where(rank_ref[:, 0, :] >= 0, 1.0, 0.0))
-
     def gram(j):
         cols = pl.ds(pl.multiple_of(j * 256, 256), 256)
         out = lax.dot_general(
             hall[:, hidden_cols(c)], hall[:, cols], (((0,), (0,)), ((), ())), preferred_element_type=F32
         )
-        gram_ref[:, cols] = out / count
+        gram_ref[:, cols] = out
 
     pl.loop(0, 6)(gram)
-    gram_copy.start()
 
     def nothing(f):
         return None
@@ -555,7 +541,6 @@
             cols = slice(cc * QUART + f * 256, cc * QUART + f * 256 + 256)
             routed = frecv[0, cc, f].astype(F32) + frecv[1, cc, f].astype(F32)
             mixed_ref[:, cols] = (stream[:, cols].astype(F32) + routed).astype(BF)
-    gram_copy.wait()
 
 
 def fused(q, ow, resid, gain, gate, rank, keys, values, wg, wu, wd):
@@ -572,7 +557,7 @@
 
     scratch = (
         [pltpu.VMEM((512, 256), BF), pltpu.VMEM((16, D), BF), pltpu.VMEM((1, D), F32), pltpu.VMEM((16, 128), F32)]
-        + [pltpu.VMEM((8, 1, 256), jnp.int32), pltpu.VMEM((FFS, FF), F32), dma((6,)), dma((1,))]
+        + [pltpu.VMEM((8, 1, 256), jnp.int32), dma((6,))]
         + [pltpu.VMEM((4, 512, HEAD_SIZE), BF), pltpu.VMEM((4, 512, 2 * HEAD_SIZE), BF), pltpu.VMEM((4, 256, 1), F32)]
         + [pltpu.VMEM((4, 256, 2 * HEAD_SIZE), F32), pltpu.VMEM((2,) * 5 + (16, 256), BF), pltpu.VMEM((8, 128, 256), BF)]
         + [pltpu.VMEM((256, D), BF)]
@@ -599,7 +584,7 @@
             jax.ShapeDtypeStruct((FFS, FF), F32),
         ),
         in_specs=[hbm] * 11,
-        out_specs=(vm, vm, hbm),
+        out_specs=(vm, vm, vm),
         scratch_shapes=scratch,
         compiler_params=pltpu.CompilerParams(
             collective_id=0, has_side_effects=True, vmem_limit_bytes=62 * 2**20
@@ -634,6 +619,7 @@
     expert = jnp.where(expert < 3 * EXPERTS, expert % EXPERTS, -1)
     gate = jnp.sum(jnp.where(own_idx[:, :, None] == expert[None, None, :], gates[:, :, None], 0.0), axis=1)
     member = jnp.any(route_idx == exp_pos, axis=1)
+    count = jnp.sum(member.astype(F32))
     member = gathered_order(member.astype(BF)).reshape(128, 16)
     before = (jnp.arange(16)[:, None] < jnp.arange(16)[None, :]).astype(BF)
     rank = jnp.dot(member, before, preferred_element_type=F32)
@@ -641,7 +627,7 @@
     mixed, attn_out, gram = fused(
         query, out_weight, resid, post_gain.reshape(1, D), gate, rank, keys, values, w_gate[0], w_up[0], w_down[0]
     )
-    return (mixed, attn_out, gram[None])
+    return (mixed, attn_out, (gram / count)[None])
 
 
 def solution(mesh):

time: 197 us -> 173 us (0.88)
  Pallas kernels: 185 us -> 161 us
  local copies, waits for them, and re-layouts: 9.59 us -> 4.49 us
  other arithmetic: 1.65 us -> 6.29 us
    pallas_call x1, Pallas kernels: 185 us -> 161 us  [fused(): pl.pallas_call(kernel, out_shape=(jax.ShapeDtypeStruct((16, D), BF), jax....]
    unnamed x7 -> x10, local copies, waits for them, and re-layouts: 7.24 us -> 2.15 us
    broadcast_in_dim x0 -> x1, other arithmetic: none -> 3.97 us  [local(): return (mixed, attn_out, (gram / count)[None])]
where the time goes in v5:
time: 173 us
  Pallas kernels  161 us (93%)
  other arithmetic  6.29 us (4%)
  local copies, waits for them, and re-layouts  4.49 us (3%)
    pallas_call x1, Pallas kernels, fused(): pl.pallas_call(kernel, out_shape=(jax.ShapeDtypeStruct((16, D), BF), jax....  161 us
    broadcast_in_dim x1, other arithmetic, local(): return (mixed, attn_out, (gram / count)[None])  3.97 us

profile of v5, /device:TPU:1, one launch (start us, length us, event | category | flops | bytes accessed | tf_op | source)
XLA Modules:
  0.0 172.8 jit_solution(16015324521753043165)
XLA Ops:
  0.6 0.9 compare_reduce_fusion
  1.5 0.7 convert_reduce_fusion
  2.2 0.8 constant_dynamic-slice_fusion
  3.0 0.1 copy.31
  3.0 0.8 copy.32
  3.8 0.7 select_reduce_fusion.gate_hbm
  4.5 0.1 reshape.37
  4.6 0.1 slice.53
  4.7 0.1 slice.51
  4.8 0.1 slice.49
  4.9 0.1 slice.47
  5.2 0.1 reshape_reshape.3
  5.3 0.1 copy.37
  5.3 0.2 fusion
  5.5 0.1 copy.38
  5.7 0.7 reshape.38.rank_hbm
  6.4 161.1 %layer.1 = (bf16[16,4096]{1,0:T(8,128)(2,1)}, f32[16,4096]{1,0:T(8,128)}, f32[384,1536]{1,0:T(8,128)}) custom-call(bf16[512,256]{1,0:T(8,128)(2,1)} %q_hbm.1, bf16[256,4096]{1,0:T(8,128)(2,1)} %ow_hbm.1, bf16[16,4096]{1,0:T(8,128)(2,1)} %resid_hbm.1, f32[1,4096]{1,0:T(1,128)} %bitcast.12, f32[16,128]{1,0:T(8,128)} %select_reduce_fusion.gate_hbm, ...), custom_call_target="tpu_custom_call" | custom-call | tf_op jit(solution)/shard_map/layer/pallas_call | solution.py:579
  167.5 0.0 copy-start.1
  167.5 0.0 copy-start
  167.5 4.0 %divide_bitcast_fusion = f32[1,384,1536]{2,1,0:T(8,128)} fusion(f32[384,1536]{1,0:T(8,128)} %get-tuple-element.8, f32[]{:T(128)} %convert_reduce_fusion), kind=kLoop, calls=%fused_computation | loop fusion | flops 589824 | bytes 4718596 | tf_op jit(solution)/shard_map/broadcast_in_dim | solution.py:630
  171.5 0.0 copy-done.1
  171.5 0.7 copy.45
  172.1 0.0 copy-done
  172.1 0.7 copy.46
  (17 shorter events, 0.2 us)
Async XLA Ops:
  167.5 4.0 %copy-start.1 = (bf16[16,4096]{1,0:T(8,128)(2,1)S(1)}, bf16[16,4096]{1,0:T(8,128)(2,1)}, u32[]{:S(2)}) copy-start(bf16[16,4096]{1,0:T(8,128)(2,1)} %get-tuple-element.20) | copy-start | bytes 393220
  167.5 4.6 %copy-start = (f32[16,4096]{1,0:T(8,128)S(1)}, f32[16,4096]{1,0:T(8,128)}, u32[]{:S(2)}) copy-start(f32[16,4096]{1,0:T(8,128)} %get-tuple-element.21) | copy-start | bytes 786436

commit v6 on v5

--- a/solution.py
+++ b/solution.py
@@ -282,7 +282,7 @@
         def _():
             kv_copy(0, sib, c, j).wait_send()
 
-    def run_rs(buf, recv, ss, rs, wait_first, steps, tail):
+    def run_rs(buf, recv, ss, rs, wait_first, steps, tail, beside):
         last = [None] * 4
         for s in range(steps):
             for f in range(4):
@@ -298,6 +298,7 @@
                 rs_add(buf, recv, f, s, own5[d])
                 if s + 1 == steps:
                     tail(f)
+            beside(s)
 
     tails = []
 
@@ -309,7 +310,7 @@
             cp.start()
             tails.append(cp)
 
-    run_rs(p1, recv1, s1s, s1r, lambda f: first[f].wait(), 3, direct)
+    run_rs(p1, recv1, s1s, s1r, lambda f: first[f].wait(), 3, direct, lambda s: None)
     parts = []
     for f in range(4):
         for i in range(3):
@@ -513,12 +514,16 @@
         )
         gram_ref[:, cols] = out
 
-    pl.loop(0, 6)(gram)
+    pl.loop(0, 2)(gram)
 
     def nothing(f):
         return None
 
-    run_rs(p2, recv2, s2s, s2r, wait_half, 4, nothing)
+    def gram_part(s):
+        if s < 2:
+            pl.loop(s * 2 + 2, s * 2 + 4)(gram)
+
+    run_rs(p2, recv2, s2s, s2r, wait_half, 4, nothing, gram_part)
     final = []
     for i, (to, (flip_l, flip_h, flip_k)) in enumerate(
         (

time: 173 us -> 174 us (level)
  no operation moved by 1% of the time
where the time goes in v6:
time: 174 us; the launch traced here: 173 us
  Pallas kernels  162 us (93%)
  other arithmetic  6.29 us (4%)
  local copies, waits for them, and re-layouts  4.49 us (3%)
    pallas_call x1, Pallas kernels, fused(): pl.pallas_call(kernel, out_shape=(jax.ShapeDtypeStruct((16, D), BF), jax....  162 us
    broadcast_in_dim x1, other arithmetic, local(): return (mixed, attn_out, (gram / count)[None])  3.97 us

profile of v6, /device:TPU:1, one launch (start us, length us, event | category | flops | bytes accessed | tf_op | source)
XLA Modules:
  0.0 173.2 jit_solution(3466553354387633618)
XLA Ops:
  0.6 0.9 compare_reduce_fusion
  1.5 0.7 convert_reduce_fusion
  2.2 0.8 constant_dynamic-slice_fusion
  3.0 0.1 copy.31
  3.0 0.8 copy.32
  3.8 0.7 select_reduce_fusion.gate_hbm
  4.5 0.1 reshape.37
  4.6 0.1 slice.53
  4.7 0.1 slice.51
  4.8 0.1 slice.49
  4.9 0.1 slice.47
  5.2 0.1 reshape_reshape.3
  5.3 0.1 copy.37
  5.3 0.2 fusion
  5.5 0.1 copy.38
  5.7 0.7 reshape.38.rank_hbm
  6.4 161.5 %layer.1 = (bf16[16,4096]{1,0:T(8,128)(2,1)}, f32[16,4096]{1,0:T(8,128)}, f32[384,1536]{1,0:T(8,128)}) custom-call(bf16[512,256]{1,0:T(8,128)(2,1)} %q_hbm.1, bf16[256,4096]{1,0:T(8,128)(2,1)} %ow_hbm.1, bf16[16,4096]{1,0:T(8,128)(2,1)} %resid_hbm.1, f32[1,4096]{1,0:T(1,128)} %bitcast.12, f32[16,128]{1,0:T(8,128)} %select_reduce_fusion.gate_hbm, ...), custom_call_target="tpu_custom_call" | custom-call | tf_op jit(solution)/shard_map/layer/pallas_call | solution.py:584
  167.9 0.0 copy-start.1
  167.9 0.0 copy-start
  167.9 4.0 %divide_bitcast_fusion = f32[1,384,1536]{2,1,0:T(8,128)} fusion(f32[384,1536]{1,0:T(8,128)} %get-tuple-element.8, f32[]{:T(128)} %convert_reduce_fusion), kind=kLoop, calls=%fused_computation | loop fusion | flops 589824 | bytes 4718596 | tf_op jit(solution)/shard_map/broadcast_in_dim | solution.py:635
  171.9 0.0 copy-done.1
  171.9 0.7 copy.45
  172.5 0.0 copy-done
  172.5 0.7 copy.46
  (17 shorter events, 0.2 us)
Async XLA Ops:
  167.9 4.0 %copy-start.1 = (bf16[16,4096]{1,0:T(8,128)(2,1)S(1)}, bf16[16,4096]{1,0:T(8,128)(2,1)}, u32[]{:S(2)}) copy-start(bf16[16,4096]{1,0:T(8,128)(2,1)} %get-tuple-element.20) | copy-start | bytes 393220
  167.9 4.6 %copy-start = (f32[16,4096]{1,0:T(8,128)S(1)}, f32[16,4096]{1,0:T(8,128)}, u32[]{:S(2)}) copy-start(f32[16,4096]{1,0:T(8,128)} %get-tuple-element.21) | copy-start | bytes 786436
